TPU v7x, 128 devices: a whole 4x4x4 slice. The times are simulated.
128 devices in a mesh: col: 8 (over x, y_lo), row: 8 (over z, core), sec: 2 (over y_hi).
Axes of the slice: x: 4, y: 4 (y_hi: 2, y_lo: 2; y = y_hi * 2 + y_lo), z: 4, core: 2. Of those that a mesh axis runs over, the one named last changes fastest.
Arguments:
- corner_left: bfloat16 [8, 8, 256, 256], P('col', 'row'), may hold values from -6 to 6
- corner_right: bfloat16 [8, 8, 256, 256], P('col', 'row'), may hold values from -6 to 6
- edge_top: bfloat16 [8, 8, 256, 100, 256], P('col', 'row', None, 'sec'), may hold values from -0.375 to 0.375
- proj_left: bfloat16 [8, 8, 256, 100, 256], P('col', 'row', None, 'sec')
- proj_right: bfloat16 [8, 8, 100, 256, 256], P('col', 'row', 'sec')
- row_order: int32 [8, 8, 2, 12800], P('col', 'row', 'sec'), may hold values from 0 to 12799, each once within a row
- block_size: int32 [8, 8, 2, 128], P('col', 'row', 'sec'), may hold values from 1 to 128, 12800 in all within a row
- block_sector: int32 [8, 8, 2, 128, 1], P('col', 'row', 'sec'), may hold values from 0 to 15; in each aligned block of 128 rows (0 to 127, 128 to 255, ..., all dimensions but the last counted through in order) at most 12 rows name the same one
- sector_owner: int32 [16], replicated, may hold values from 0 to 15, each once
Outputs:
- new_left: float32 [8, 8, 256, 256], P('col', 'row')
- new_right: float32 [8, 8, 256, 256], P('col', 'row')
- sector_gram: float32 [8, 16, 256, 256], P('col', ('row', 'sec'))
Inputs may be any that keep to these rules, and one draw needn't show every extreme that they name: `block_sector`: within the rows of one device (one site and part) no sector has more than 12 blocks, and some sector has exactly 12. `block_size`: sizes of a part's blocks sum to 12800. `row_order`: each part's rows appear once. `sector_owner`: each owner holds one sector.
All inputs are finite; a program needn't handle non-finite values.
Results may differ from a plain program's by a relative error of at most 0.0029.
Values may be sent and summed in bfloat16 or wider, within the bound.
A program may use at most 192 MiB of HBM per device.

v0:
```python
import jax
import jax.numpy as jnp
from jax import lax
from jax.sharding import PartitionSpec as P

BLK = 128


epsilon = 1e-06


def from_behind(value, axis, steps):
    count = lax.axis_size(axis)
    pairs = [(source, (source + steps) % count) for source in range(count)]
    return lax.ppermute(value, axis, pairs)


def slot_table(row_perm, lengths, owners_of_block, count_owners, capacity, width):
    block_count = lengths.shape[0]
    total_rows = row_perm.shape[0]
    starts = jnp.cumsum(lengths) - lengths
    block_ids = jnp.arange(block_count, dtype=jnp.int32)
    same_owner = owners_of_block[:, None] == owners_of_block[None, :]
    earlier = block_ids[None, :] < block_ids[:, None]
    slot_rank = jnp.sum((same_owner & earlier).astype(jnp.int32), axis=1)
    owner_ids = jnp.arange(count_owners, dtype=jnp.int32)[:, None, None]
    slot_ids = jnp.arange(capacity, dtype=jnp.int32)[None, :, None]
    matched = (
        (owners_of_block[None, None, :] == owner_ids) & (slot_rank[None, None, :] == slot_ids)
    ).astype(jnp.int32)
    slot_start = jnp.sum(matched * starts[None, None, :], axis=2)
    slot_size = jnp.sum(matched * lengths[None, None, :], axis=2)
    offsets = jnp.arange(width, dtype=jnp.int32)
    usable = offsets[None, None, :] < slot_size[:, :, None]
    position = jnp.minimum(slot_start[:, :, None] + offsets[None, None, :], total_rows - 1)
    return jnp.where(usable, jnp.take(row_perm, position), total_rows)


def slot_grams(received):
    return jnp.einsum("scra,scrb->cab", received, received, preferred_element_type=jnp.float32)


def body(
    corner_left,
    corner_right,
    edge_top,
    proj_left,
    proj_right,
    row_order,
    block_size,
    block_sector,
    sector_owner,
):
    from_left = from_behind(corner_left, "col", 1)[0, 0]
    from_right = from_behind(corner_right, "col", -1)[0, 0]
    top_edge = edge_top[0, 0]
    bond_dim = top_edge.shape[0]
    joined_rows = top_edge.shape[0] * top_edge.shape[1]
    enlarged = jnp.einsum(
        "ab,buc->auc", from_left, top_edge, preferred_element_type=jnp.float32
    ).astype(jnp.bfloat16)
    enlarged_rows = enlarged.reshape(joined_rows, bond_dim)
    left_part = lax.dot_general(
        proj_left[0, 0].reshape(joined_rows, bond_dim),
        enlarged_rows,
        (((0,), (0,)), ((), ())),
        preferred_element_type=jnp.float32,
    )
    right_big = jnp.einsum(
        "buc,ca->bua", top_edge, from_right, preferred_element_type=jnp.float32
    ).astype(jnp.bfloat16)
    right_part = jnp.einsum(
        "bua,uap->bp", right_big, proj_right[0, 0], preferred_element_type=jnp.float32
    )
    row_perm = row_order[0, 0, 0]
    lengths = block_size[0, 0, 0]
    sectors = block_sector[0, 0, 0, :, 0]
    count_owners = lax.axis_size(("row", "sec"))
    block_count = lengths.shape[0]
    sector_ids = jnp.arange(count_owners, dtype=jnp.int32)
    owners_of_block = jnp.sum(
        jnp.where(sectors[:, None] == sector_ids[None, :], sector_owner[None, :], 0), axis=1
    )
    capacity = 3 * block_count // (2 * count_owners)
    slot_rows = slot_table(row_perm, lengths, owners_of_block, count_owners, capacity, BLK)
    outgoing = jnp.take(enlarged_rows, slot_rows, axis=0, mode="fill", fill_value=0)
    per_slot = slot_grams(
        lax.all_to_all(outgoing, ("row", "sec"), split_axis=0, concat_axis=0, tiled=True)
    )
    sector_gram = jnp.sum(per_slot, axis=0)[None, None]
    left_sum, right_sum = lax.psum((left_part, right_part), "sec")
    new_left = left_sum * lax.rsqrt(jnp.mean(left_sum * left_sum) + epsilon)
    new_right = right_sum * lax.rsqrt(jnp.mean(right_sum * right_sum) + epsilon)
    return (new_left[None, None], new_right[None, None], sector_gram)


def solution(mesh):
    in_specs = (
        P("col", "row", None, None),
        P("col", "row", None, None),
        P("col", "row", None, "sec", None),
        P("col", "row", None, "sec", None),
        P("col", "row", "sec", None, None),
        P("col", "row", "sec", None),
        P("col", "row", "sec", None),
        P("col", "row", "sec", None, None),
        P(),
    )
    out_specs = (
        P("col", "row", None, None),
        P("col", "row", None, None),
        P("col", ("row", "sec"), None, None),
    )
    return jax.shard_map(body, mesh=mesh, in_specs=in_specs, out_specs=out_specs, check_vma=False)
```

profile of v0, /device:TPU:0, one launch (start us, length us, event | category | flops | bytes accessed | tf_op | source)
XLA Modules:
  0.0 508.1 jit_solution(3616110388788631576)
XLA Ops:
  7.2 0.0 copy-start
  7.2 1.7 collective-permute-start
  8.9 0.8 select_reduce_fusion
  9.7 0.2 convert_reduce_fusion
  9.9 0.8 copy.22
  10.6 0.0 copy-done
  10.6 0.1 reduce.1
  10.8 0.2 reduce-window.8
  10.9 0.1 reduce
  11.1 0.7 bitcast_subtract_fusion
  11.7 1.3 fusion.11
  13.0 0.1 compare_select_fusion.2
  13.2 135.5 %gather_fusion = s32[24576]{0:T(1024)S(1)} fusion(s32[12800]{0:T(1024)S(1)} %reduce.1, s32[24576]{0:T(1024)S(1)} %broadcast_clamp_fusion.1), kind=kCustom, calls=%fused_computation | custom fusion | bytes 294912 | tf_op jit(solution)/shard_map/jit(_take)/gather | solution.py:36
  148.7 0.1 compare_select_fusion
  148.9 0.2 compare_and_fusion
  149.1 0.0 collective-permute-done
  149.1 4.7 convolution_convert_fusion.1
  153.8 6.9 %copy.20 = bf16[256,50,256]{2,1,0:T(8,128)(2,1)} copy(bf16[256,50,256]{2,0,1:T(8,128)(2,1)S(1)} %convolution_convert_fusion.1) | data formatting | bytes 13107200 | tf_op jit(solution)/shard_map/convert_element_type | solution.py:61
  160.7 10.7 %reshape.155 = bf16[12800,256]{1,0:T(8,128)(2,1)} reshape(bf16[256,50,256]{2,1,0:T(8,128)(2,1)} %copy.20) | data formatting | bytes 13107200 | tf_op jit(solution)/shard_map/reshape | solution.py:62
  171.5 94.5 %gather_fusion.1 = bf16[24576,256]{1,0:T(8,128)(2,1)} fusion(bf16[12800,256]{1,0:T(8,128)(2,1)} %reshape.155, s32[24576]{0:T(1024)S(1)} %broadcast_clamp_fusion), kind=kCustom, calls=%fused_computation.1 | custom fusion | bytes 25264128 | tf_op jit(solution)/shard_map/jit(_take)/gather | solution.py:86
  265.9 10.9 %broadcast_select_fusion = bf16[16,12,128,256]{3,2,1,0:T(8,128)(2,1)} fusion(bf16[16,12,128,256]{3,2,1,0:T(8,128)(2,1)} %bitcast.52, pred[16,12,128]{2,1,0:T(8,128)(4,1)S(1)} %compare_and_fusion), kind=kLoop, calls=%fused_computation.2 | loop fusion | flops 6291456 | bytes 25190400 | tf_op jit(solution)/shard_map/jit(_take)/select_n | solution.py:86
  276.8 0.0 copy-start.2
  276.8 7.9 %all-to-all-start = ((bf16[16,12,128,256]{3,2,1,0:T(8,128)(2,1)}), bf16[16,12,128,256]{3,2,1,0:T(8,128)(2,1)}, u32[]{:S(2)}, u32[]{:S(2)}) async-start(bf16[16,12,128,256]{3,2,1,0:T(8,128)(2,1)} %broadcast_select_fusion), calls=%async_computation | async-start | bytes 25165824 | tf_op jit(solution)/shard_map/all_to_all | solution.py:88
  284.8 0.0 all-reduce.3.cloned.1.call-start
  284.8 0.0 copy-done.2
  284.8 2.5 collective-permute-start.1
  287.3 9.7 %copy.21 = bf16[1,1,256,50,256]{4,3,2,1,0:T(8,128)(2,1)} copy(bf16[1,1,256,50,256]{4,2,3,1,0:T(8,128)(2,1)} %param.12) | data formatting | bytes 13107200 | tf_op args[3]
  297.0 10.7 %reshape_squeeze.3 = bf16[12800,256]{1,0:T(8,128)(2,1)} reshape(bf16[1,1,256,50,256]{4,3,2,1,0:T(8,128)(2,1)} %copy.21) | data formatting | bytes 13107200 | tf_op jit(solution)/shard_map/reshape;squeeze | solution.py:64
  307.7 118.3 %collective-permute-done.1 = bf16[1,1,256,256]{3,2,1,0:T(8,128)(2,1)S(1)} collective-permute-done((bf16[1,1,256,256]{3,2,1,0:T(8,128)(2,1)S(1)}, bf16[1,1,256,256]{3,2,1,0:T(8,128)(2,1)S(1)}, u32[]{:S(2)}, u32[]{:S(2)}) %collective-permute-start.1) | collective-permute-done | bytes 131104 | tf_op jit(solution)/shard_map/ppermute | solution.py:15
  426.0 9.3 %fusion.6 = f32[256,256]{1,0:T(8,128)} fusion(bf16[1,1,50,256,256]{4,3,2,1,0:T(8,128)(2,1)} %param.13, bf16[1,1,256,50,256]{4,2,3,1,0:T(8,128)(2,1)} %param.11, bf16[1,1,256,256]{3,2,1,0:T(8,128)(2,1)S(1)} %collective-permute-done.1), kind=kOutput, calls=%fused_computation.9 | convolution fusion | flops 3358720000 | bytes 13500416 | tf_op jit(solution)/shard_map/bua,uap->bp/dot_general | solution.py:72
  435.3 7.3 %convolution_bitcast_fusion.1 = f32[256,256]{0,1:T(8,128)} fusion(bf16[12800,256]{1,0:T(8,128)(2,1)} %reshape.155, bf16[12800,256]{1,0:T(8,128)(2,1)} %reshape_squeeze.3), kind=kOutput, calls=%fused_computation.11 | convolution fusion | flops 1677721600 | bytes 13369344 | tf_op jit(solution)/shard_map/dot_general | solution.py:63
  442.7 0.0 all-reduce.3.cloned.1.call-update
  442.7 38.1 %all-reduce.3.cloned.1.call-done = (f32[256,256]{0,1:T(8,128)}, f32[256,256]{1,0:T(8,128)}) async-done(((f32[256,256]{0,1:T(8,128)}, f32[256,256]{1,0:T(8,128)}), (f32[256,256]{0,1:T(8,128)}, f32[256,256]{1,0:T(8,128)})) %all-reduce.3.cloned.1.call-update) | async-done | bytes 524304 | tf_op jit(solution)/shard_map/psum | solution.py:91
  480.8 1.6 multiply_reduce_fusion
  483.1 1.6 multiply_reduce_fusion.1
  485.5 1.0 multiply_bitcast_fusion.1
  486.4 0.8 copy.24
  487.3 1.7 multiply_bitcast_fusion
  488.9 0.0 all-to-all-done
  488.9 0.0 copy-start.1
  488.9 12.3 %convolution_bitcast_fusion = f32[1,1,256,256]{3,2,1,0:T(8,128)} fusion(bf16[16,12,128,256]{3,2,1,0:T(8,128)(2,1)} %all-to-all-done), kind=kOutput, calls=%fused_computation.10 | convolution fusion | flops 3221225472 | bytes 12845056 | tf_op jit(solution)/shard_map/scra,scrb->cab/dot_general | solution.py:40
  501.2 0.0 copy-done.1
  (8 shorter events, 0.1 us)
Async XLA Ops:
  7.2 3.5 copy-start
  7.2 141.9 %collective-permute-start = (bf16[1,1,256,256]{3,2,1,0:T(8,128)(2,1)}, bf16[1,1,256,256]{3,2,1,0:T(8,128)(2,1)S(1)}, u32[]{:S(2)}, u32[]{:S(2)}) collective-permute-start(bf16[1,1,256,256]{3,2,1,0:T(8,128)(2,1)} %param.9), channel_id=1, source_target_pairs={{0,16},{16,32},{32,48},{48,64},{64,80},{80,96},{96,112},{112,0},{1... | collective-permute-start | bytes 393224 | tf_op jit(solution)/shard_map/ppermute | solution.py:15
  276.8 8.0 %copy-start.2 = (bf16[1,1,256,256]{3,2,1,0:T(8,128)(2,1)S(1)}, bf16[1,1,256,256]{3,2,1,0:T(8,128)(2,1)}, u32[]{:S(2)}) copy-start(bf16[1,1,256,256]{3,2,1,0:T(8,128)(2,1)} %param.10) | copy-start | bytes 393220
  276.8 212.1 %all-to-all-start = ((bf16[16,12,128,256]{3,2,1,0:T(8,128)(2,1)}), bf16[16,12,128,256]{3,2,1,0:T(8,128)(2,1)}, u32[]{:S(2)}, u32[]{:S(2)}) async-start(bf16[16,12,128,256]{3,2,1,0:T(8,128)(2,1)} %broadcast_select_fusion), calls=%async_computation | async-start | bytes 25165824 | tf_op jit(solution)/shard_map/all_to_all | solution.py:88
  284.8 196.1 %all-reduce.3.cloned.1.call-start = ((), (), s32[]{:S(2)}) async-start(), calls=%async_computation.1 | async-start | bytes 1048576 | tf_op jit(solution)/shard_map/psum | solution.py:91
  284.8 141.2 %collective-permute-start.1 = (bf16[1,1,256,256]{3,2,1,0:T(8,128)(2,1)S(1)}, bf16[1,1,256,256]{3,2,1,0:T(8,128)(2,1)S(1)}, u32[]{:S(2)}, u32[]{:S(2)}) collective-permute-start(bf16[1,1,256,256]{3,2,1,0:T(8,128)(2,1)S(1)} %copy-done.2), channel_id=1, source_target_pairs={{0,112},{16,0},{32,16},{48,32},{64,48},{80,64},{96,80},{112,96},{1... | collective-permute-start | bytes 393224 | tf_op jit(solution)/shard_map/ppermute | solution.py:15
  488.9 12.3 %copy-start.1 = (s32[1,1,1,12800]{3,2,1,0:T(1,128)S(1)}, s32[1,1,1,12800]{3,2,1,0:T(1,128)}, u32[]{:S(2)}) copy-start(s32[1,1,1,12800]{3,2,1,0:T(1,128)} %param.14) | copy-start | bytes 153604
Sparse Core Ops, SparseCore 0:
  442.8 37.9 all-reduce.2
where the time goes:
time: 510 us; the launch traced here: 508 us
  local copies, waits for them, and re-layouts  270 us (53%)
  waiting for transfers between devices  156 us (31%)
  matrix products  33.7 us (7%)
  other arithmetic  20.5 us (4%)
  between operations  15.6 us (3%)
  starting transfers between devices  12.2 us (2%)
    gather x3, local copies, waits for them, and re-layouts, slot_table(): return jnp.where(usable, jnp.take(row_perm, position), total_rows)  136 us
    ppermute x2, waiting for transfers between devices, from_behind(): return lax.ppermute(value, axis, pairs)  118 us
    gather x1, local copies, waits for them, and re-layouts, body(): jnp.take(enlarged_rows, slot_rows, axis=0, mode='fill', fill_value=0)  94.5 us
    psum x1, waiting for transfers between devices, body(): left_sum, right_sum = lax.psum((left_part, right_part), 'sec')  38.1 us
    dot_general x1, matrix products, slot_grams(): jnp.einsum('scra,scrb->cab', received, received, preferred_element_type=j...  12.3 us
    select_n x2, other arithmetic, body(): jnp.take(enlarged_rows, slot_rows, axis=0, mode='fill', fill_value=0)  11 us
    reshape x1, local copies, waits for them, and re-layouts, body(): enlarged_rows = enlarged.reshape(joined_rows, bond_dim)  10.7 us
    another operation x1, local copies, waits for them, and re-layouts, body(): proj_left[0, 0].reshape(joined_rows, bond_dim)  10.7 us
  transfers between devices with their start and end apart: 4, of which 2 were waited for; matrix products, arithmetic and copies ran while one was open for 36% of the time, Pallas kernels for 0%

commit v1 on v0

v1 whole, which is shorter than its diff:
```python
import functools

import jax
import jax.numpy as jnp
from jax import lax
from jax.experimental import pallas as pl
from jax.experimental.pallas import tpu as pltpu
from jax.sharding import PartitionSpec as P

CHI = 256
UNITS = 50
OWNERS = 16
LANES = 128
TILE = 16
TILES = 32
CAP_TILES = 144
DUMP = OWNERS * CAP_TILES
GROUP = 5
GRAM_TILES = 48
EPSILON = 1e-06

F32 = jnp.float32
BF16 = jnp.bfloat16


def dot(x, y):
    return lax.dot_general(x, y, (((1,), (0,)), ((), ())), preferred_element_type=F32)


def dot_nt(x, y):
    return lax.dot_general(x, y, (((1,), (1,)), ((), ())), preferred_element_type=F32)


def dot_tn(x, y):
    return lax.dot_general(x, y, (((0,), (0,)), ((), ())), preferred_element_type=F32)


def iota(shape, axis):
    return lax.broadcasted_iota(jnp.int32, shape, axis)


def ones_where(mask):
    return jnp.where(mask, 1.0, 0.0).astype(BF16)


def plan_kernel(owner_ref, order_ref, size_ref, sector_ref, dest_ref, place_ref, count_ref):
    sector = sector_ref[...]
    named = jnp.zeros((1, LANES), F32)
    for s in range(OWNERS):
        named = jnp.where(sector == s, (owner_ref[s] + 1).astype(F32), named)
    up = iota((LANES, LANES), 0)
    across = iota((LANES, LANES), 1)
    before = ones_where(up < across)
    steps = ones_where(up == across) - ones_where(up + 1 == across)
    sizes = jnp.broadcast_to(size_ref[...].astype(F32), (8, LANES)).astype(BF16)
    starts = dot(sizes, before)[0:1]
    delta = dot(jnp.broadcast_to(named, (8, LANES)).astype(BF16), steps)[0:1]
    start_hi = jnp.floor((starts + 0.5) * (1.0 / LANES))
    start_lo = starts - LANES * start_hi
    place_hi = iota((104, LANES), 0).astype(F32)
    impulses = dot_nt(
        jnp.where(place_hi == start_hi, delta, 0.0).astype(BF16),
        ones_where(up.astype(F32) == start_lo),
    ).astype(BF16)
    inside = dot(impulses, ones_where(up <= across))
    totals = jnp.broadcast_to(inside[:, LANES - 1:LANES], (104, LANES)).astype(BF16)
    earlier = ones_where(iota((104, 104), 1) < iota((104, 104), 0))
    listed = inside + dot(earlier, totals)
    order = order_ref[...].astype(F32)
    bond = jnp.floor((order + 0.5) * (1.0 / UNITS))
    unit = order - UNITS * bond
    bonds = iota((CHI, LANES), 0).astype(F32)
    units = iota((64, LANES), 0).astype(F32)
    owned = jnp.zeros((64, CHI), F32)
    for first in range(0, 100, 10):
        left, right = [], []
        for h in range(first, first + 10):
            left.append(jnp.where(units == unit[h:h + 1], listed[h:h + 1], 0.0).astype(BF16))
            right.append(ones_where(bonds == bond[h:h + 1]))
        owned = owned + dot_nt(jnp.concatenate(left, axis=1), jnp.concatenate(right, axis=1))
    hits = [owned == float(o + 1) for o in range(OWNERS)]
    onehot = [ones_where(hit) for hit in hits]
    lower = ones_where(iota((CHI, CHI), 0) < iota((CHI, CHI), 1))
    offset = jnp.zeros((64, 1), F32)
    dest = jnp.full((64, CHI), -1.0, F32)
    lane = iota((64, LANES), 1)
    tile_counts = jnp.zeros((64, LANES), F32)
    offsets, counts = [], []
    for o in range(OWNERS):
        rank = dot(onehot[o], lower)
        amount = rank[:, CHI - 1:CHI] + onehot[o].astype(F32)[:, CHI - 1:CHI]
        tiles = jnp.floor((amount + (TILE - 1)) * (1.0 / TILE))
        dest = jnp.where(hits[o], TILE * offset + rank, dest)
        tile_counts = jnp.where(lane == o, tiles, tile_counts)
        offsets.append(offset)
        counts.append(tiles)
        offset = offset + tiles
    dest_ref[...] = dest
    earlier = ones_where(iota((64, 64), 1) < iota((64, 64), 0))
    sofar = dot(earlier, tile_counts.astype(BF16))
    slot = lane.astype(F32)
    place = jnp.full((64, LANES), float(DUMP), F32)
    for o in range(OWNERS):
        mine = (slot >= offsets[o]) & (slot < offsets[o] + counts[o])
        place = jnp.where(mine, sofar[:, o:o + 1] - offsets[o] + slot + float(o * CAP_TILES), place)
    place_ref[...] = place.astype(jnp.int32)
    count_ref[...] = jnp.sum(tile_counts, axis=0, keepdims=True).astype(jnp.int32)


def plan(sector_owner, row_order, block_size, block_sector):
    vmem = pl.BlockSpec(memory_space=pltpu.VMEM)
    return pl.pallas_call(
        plan_kernel,
        out_shape=(
            jax.ShapeDtypeStruct((64, CHI), F32),
            jax.ShapeDtypeStruct((64, LANES), jnp.int32),
            jax.ShapeDtypeStruct((1, LANES), jnp.int32),
        ),
        in_specs=[pl.BlockSpec(memory_space=pltpu.SMEM), vmem, vmem, vmem],
        out_specs=(vmem, vmem, vmem),
        cost_estimate=pl.CostEstimate(flops=2 * 64 * 12800 * 256, bytes_accessed=200000, transcendentals=0),
        compiler_params=pltpu.CompilerParams(vmem_limit_bytes=32 * 1024 * 1024),
    )(sector_owner, row_order, block_size, block_sector)


def site_kernel(
    place_ref, count_ref, dest_ref, left_ref, right_ref, edge_ref, proj_left_ref, proj_right_ref,
    out_left, out_right, out_gram, enlarged, wide, buckets,
):
    step = pl.program_id(0)

    @pl.when(step == 0)
    def _():
        out_left[...] = jnp.zeros_like(out_left)
        out_right[...] = jnp.zeros_like(out_right)

    slots = iota((TILES * TILE, CHI), 0).astype(F32)
    for j in range(GROUP):
        rows = pl.ds(j * CHI, CHI)
        enlarged[rows, :] = dot(left_ref[...], edge_ref[j]).astype(BF16)
        wide[:, rows] = dot(edge_ref[j], right_ref[...]).astype(BF16)
    out_left[...] += dot_tn(proj_left_ref[...].reshape(GROUP * CHI, CHI), enlarged[...])
    out_right[...] += dot(wide[...], proj_right_ref[...].reshape(GROUP * CHI, CHI))
    for j in range(GROUP):
        u = step * GROUP + j
        pick = ones_where(slots == dest_ref[pl.ds(u, 1), :])
        sorted_rows = dot(pick, enlarged[pl.ds(j * CHI, CHI), :]).astype(BF16)
        for t in range(TILES - 1):
            at = pl.multiple_of(place_ref[u, t] * TILE, TILE)
            buckets[pl.ds(at, TILE), :] = sorted_rows[t * TILE:(t + 1) * TILE]

    @pl.when(step == UNITS // GROUP - 1)
    def _():
        @pl.loop(0, OWNERS)
        def _(o):
            total = count_ref[0, o]
            products = (total + (GRAM_TILES - 1)) // GRAM_TILES
            base = o * CAP_TILES

            @pl.loop(total, products * GRAM_TILES)
            def _(t):
                at = pl.multiple_of((base + t) * TILE, TILE)
                buckets[pl.ds(at, TILE), :] = jnp.zeros((TILE, CHI), BF16)

            out_gram[o] = jnp.zeros((CHI, CHI), F32)

            @pl.loop(0, products)
            def _(k):
                at = pl.multiple_of((base + k * GRAM_TILES) * TILE, TILE)
                rows = buckets[pl.ds(at, GRAM_TILES * TILE), :]
                out_gram[o] += dot_tn(rows, rows)


def site(place, count, dest, from_left, from_right, edge, proj_left, proj_right):
    whole = lambda shape: pl.BlockSpec(shape, lambda i, *_: (0,) * len(shape))
    group = pl.BlockSpec((GROUP, CHI, CHI), lambda i, *_: (i, 0, 0))
    return pl.pallas_call(
        site_kernel,
        grid_spec=pltpu.PrefetchScalarGridSpec(
            num_scalar_prefetch=2,
            grid=(UNITS // GROUP,),
            in_specs=[whole((64, CHI)), whole((CHI, CHI)), whole((CHI, CHI)), group, group, group],
            out_specs=[whole((CHI, CHI)), whole((CHI, CHI)), whole((OWNERS, CHI, CHI))],
            scratch_shapes=[
                pltpu.VMEM((GROUP * CHI, CHI), BF16),
                pltpu.VMEM((CHI, GROUP * CHI), BF16),
                pltpu.VMEM(((DUMP + 1) * TILE, CHI), BF16),
            ],
        ),
        out_shape=(
            jax.ShapeDtypeStruct((CHI, CHI), F32),
            jax.ShapeDtypeStruct((CHI, CHI), F32),
            jax.ShapeDtypeStruct((OWNERS, CHI, CHI), F32),
        ),
        cost_estimate=pl.CostEstimate(flops=8 * 2 * 12800 * 65536, bytes_accessed=24 << 20, transcendentals=0),
        compiler_params=pltpu.CompilerParams(vmem_limit_bytes=56 * 1024 * 1024),
    )(place, count, dest, from_left, from_right, edge, proj_left, proj_right)


def from_behind(value, axis, steps):
    count = lax.axis_size(axis)
    pairs = [(source, (source + steps) % count) for source in range(count)]
    return lax.ppermute(value, axis, pairs)


def body(
    corner_left, corner_right, edge_top, proj_left, proj_right, row_order, block_size, block_sector, sector_owner,
):
    from_left = from_behind(corner_left, "col", 1)[0, 0]
    from_right = from_behind(corner_right, "col", -1)[0, 0]
    dest, place, count = plan(
        sector_owner,
        row_order.reshape(100, LANES),
        block_size.reshape(1, LANES),
        block_sector.reshape(1, LANES),
    )
    edge = jnp.transpose(edge_top[0, 0], (1, 0, 2))
    left = jnp.transpose(proj_left[0, 0], (1, 0, 2))
    left_part, right_part, grams = site(place, count, dest, from_left, from_right, edge, left, proj_right[0, 0])
    parts = lax.all_to_all(grams.astype(BF16), ("row", "sec"), split_axis=0, concat_axis=0, tiled=True)
    sector_gram = jnp.sum(parts.astype(F32), axis=0)[None, None]
    left_sum, right_sum = lax.psum((left_part, right_part), "sec")
    new_left = left_sum * lax.rsqrt(jnp.mean(left_sum * left_sum) + EPSILON)
    new_right = right_sum * lax.rsqrt(jnp.mean(right_sum * right_sum) + EPSILON)
    return (new_left[None, None], new_right[None, None], sector_gram)


def solution(mesh):
    in_specs = (
        P("col", "row", None, None),
        P("col", "row", None, None),
        P("col", "row", None, "sec", None),
        P("col", "row", None, "sec", None),
        P("col", "row", "sec", None, None),
        P("col", "row", "sec", None),
        P("col", "row", "sec", None),
        P("col", "row", "sec", None, None),
        P(),
    )
    out_specs = (
        P("col", "row", None, None),
        P("col", "row", None, None),
        P("col", ("row", "sec"), None, None),
    )
    return jax.shard_map(body, mesh=mesh, in_specs=in_specs, out_specs=out_specs, check_vma=False)
```

time: 510 us -> 130 us (0.25)
  local copies, waits for them, and re-layouts: 270 us -> 4.37 us
  waiting for transfers between devices: 156 us -> 46.7 us
  Pallas kernels: 0 us -> 37.5 us
  matrix products: 33.7 us -> 0 us
  other arithmetic: 20.5 us -> 10.8 us
    gather x4 -> x0, local copies, waits for them, and re-layouts: 230 us -> none  [the longest x3 136 us: slot_table(): return jnp.where(usable, jnp.take(row_perm, position), total_rows)]
    ppermute x2, waiting for transfers between devices: 118 us -> 0.01 us  [from_behind(): return lax.ppermute(value, axis, pairs)]
    pallas_call x0 -> x2, Pallas kernels: none -> 37.5 us  [the longest x1 32.9 us: site(): pl.pallas_call(site_kernel, grid_spec=pltpu.PrefetchScalarGridSpec(num_sc...]
    dot_general x4 -> x0, matrix products: 33.7 us -> none  [the longest x1 12.3 us: slot_grams(): jnp.einsum('scra,scrb->cab', received, received, preferred_element_type=j...]
    another operation x2 -> x0, local copies, waits for them, and re-layouts: 11.5 us -> none  [the longest x1 10.7 us: body(): proj_left[0, 0].reshape(joined_rows, bond_dim)]
    select_n x3 -> x0, other arithmetic: 11.1 us -> none  [the longest x2 11 us: body(): jnp.take(enlarged_rows, slot_rows, axis=0, mode='fill', fill_value=0)]
    reshape x1 -> x0, local copies, waits for them, and re-layouts: 10.7 us -> none  [body(): enlarged_rows = enlarged.reshape(joined_rows, bond_dim)]
    psum x1, waiting for transfers between devices: 38.1 us -> 46 us  [body(): left_sum, right_sum = lax.psum((left_part, right_part), 'sec')]
  transfers between devices with their start and end apart: 4 -> 4, of which waited for: 2 -> 1; matrix products, arithmetic and copies ran while one was open for 36% -> 5% of each run, Pallas kernels for 0% -> 4%
where the time goes in v1:
time: 130 us; the launch traced here: 129 us
  waiting for transfers between devices  46.7 us (36%)
  Pallas kernels  37.5 us (29%)
  between operations  15.5 us (12%)
  starting transfers between devices  14 us (11%)
  other arithmetic  10.8 us (8%)
  local copies, waits for them, and re-layouts  4.37 us (3%)
    psum x1, waiting for transfers between devices, body(): left_sum, right_sum = lax.psum((left_part, right_part), 'sec')  46 us
    pallas_call x1, Pallas kernels, site(): pl.pallas_call(site_kernel, grid_spec=pltpu.PrefetchScalarGridSpec(num_sc...  32.9 us
    all_to_all x1, starting transfers between devices, body(): lax.all_to_all(grams.astype(BF16), ('row', 'sec'), split_axis=0, concat_a...  9.71 us
    pallas_call x1, Pallas kernels, plan(): pl.pallas_call(plan_kernel, out_shape=(jax.ShapeDtypeStruct((64, CHI), F3...  4.59 us
    unnamed x16, local copies, waits for them, and re-layouts  4.37 us
    ppermute x2, starting transfers between devices, from_behind(): return lax.ppermute(value, axis, pairs)  4.2 us
    convert_element_type x1, other arithmetic, body(): grams.astype(BF16)  3.77 us
  transfers between devices with their start and end apart: 4, of which 1 were waited for; matrix products, arithmetic and copies ran while one was open for 5% of the time, Pallas kernels for 4%

profile of v1, /device:TPU:0, one launch (start us, length us, event | category | flops | bytes accessed | tf_op | source)
XLA Modules:
  0.0 128.8 jit_solution(6907778852736091800)
XLA Ops:
  7.2 1.7 %collective-permute-start = (bf16[1,1,256,256]{3,2,1,0:T(8,128)(2,1)}, bf16[1,1,256,256]{3,2,1,0:T(8,128)(2,1)S(1)}, u32[]{:S(2)}, u32[]{:S(2)}) collective-permute-start(bf16[1,1,256,256]{3,2,1,0:T(8,128)(2,1)} %param.9), channel_id=1, source_target_pairs={{0,16},{16,32},{32,48},{48,64},{64,80},{80,96},{96,112},{112,0},{1... | collective-permute-start | bytes 393224 | tf_op jit(solution)/shard_map/ppermute | solution.py:203
  8.9 2.5 %collective-permute-start.1 = (bf16[1,1,256,256]{3,2,1,0:T(8,128)(2,1)}, bf16[1,1,256,256]{3,2,1,0:T(8,128)(2,1)S(1)}, u32[]{:S(2)}, u32[]{:S(2)}) collective-permute-start(bf16[1,1,256,256]{3,2,1,0:T(8,128)(2,1)} %param.10), channel_id=1, source_target_pairs={{0,112},{16,0},{32,16},{48,32},{64,48},{80,64},{96,80},{112,96},{1... | collective-permute-start | bytes 393224 | tf_op jit(solution)/shard_map/ppermute | solution.py:203
  11.4 0.9 reduce
  12.3 0.0 copy-start
  12.3 0.6 copy-done
  13.0 0.0 copy-start.1
  13.0 0.7 copy-done.1
  13.6 0.0 copy-start.2
  13.6 0.7 copy-done.2
  14.3 4.6 %shard_map.112 = (f32[64,256]{1,0:T(8,128)S(1)}, s32[64,128]{1,0:T(8,128)S(1)}, s32[1,128]{1,0:T(1,128)S(1)}) custom-call(s32[16]{0:T(128)S(1)} %copy-done, s32[100,128]{1,0:T(8,128)S(1)} %bitcast.17, s32[1,128]{1,0:T(1,128)S(1)} %bitcast.18, s32[1,128]{1,0:T(1,128)S(1)} %bitcast.19), custom_call_target="tpu_custom_call" | custom-call | flops 419430400 | bytes 200000 | tf_op jit(solution)/shard_map/pallas_call | solution.py:112
  18.9 0.0 copy-start.3
  18.9 0.6 copy-done.3
  19.5 0.0 copy-start.4
  19.5 0.6 copy-done.4
  20.1 0.0 copy-start.5
  20.1 0.5 copy-done.5
  20.6 0.0 collective-permute-done
  20.6 0.0 copy-start.6
  20.6 0.0 collective-permute-done.1
  20.6 0.0 copy-start.7
  20.6 0.6 copy-done.6
  21.3 0.0 copy-done.7
  21.3 32.9 %shard_map.113 = (f32[256,256]{1,0:T(8,128)}, f32[256,256]{1,0:T(8,128)}, f32[16,256,256]{2,1,0:T(8,128)}) custom-call(s32[64,128]{1,0:T(8,128)} %copy-done.4, s32[1,128]{1,0:T(1,128)} %copy-done.5, f32[64,256]{1,0:T(8,128)} %copy-done.3, bf16[256,256]{1,0:T(8,128)(2,1)} %bitcast.24, bf16[256,256]{1,0:T(8,128)(2,1)} %bitcast.25, ...), custom_call_target="tpu_custom_call" | custom-call | flops 13421772800 | bytes 25165824 | tf_op jit(solution)/shard_map/pallas_call | solution.py:177
  54.2 3.8 %convert_element_type.6 = bf16[16,256,256]{2,1,0:T(8,128)(2,1)} convert(f32[16,256,256]{2,1,0:T(8,128)} %get-tuple-element.14) | non-fusion elementwise | flops 1048576 | bytes 6291456 | tf_op jit(solution)/shard_map/convert_element_type | solution.py:220
  58.0 9.7 %all-to-all-start = ((bf16[16,256,256]{2,1,0:T(8,128)(2,1)}), bf16[16,256,256]{2,1,0:T(8,128)(2,1)S(1)}, u32[]{:S(2)}, u32[]{:S(2)}) async-start(bf16[16,256,256]{2,1,0:T(8,128)(2,1)} %convert_element_type.6), calls=%async_computation | async-start | bytes 4194304 | tf_op jit(solution)/shard_map/all_to_all | solution.py:220
  67.7 0.0 all-reduce.3.cloned.1.call-start
  67.7 0.7 all-reduce.3.cloned.1.call-update
  68.4 46.0 %all-reduce.3.cloned.1.call-done = (f32[256,256]{1,0:T(8,128)}, f32[256,256]{1,0:T(8,128)}) async-done(((f32[256,256]{1,0:T(8,128)}, f32[256,256]{1,0:T(8,128)}), (f32[256,256]{1,0:T(8,128)}, f32[256,256]{1,0:T(8,128)})) %all-reduce.3.cloned.1.call-update) | async-done | bytes 524304 | tf_op jit(solution)/shard_map/psum | solution.py:222
  114.5 1.6 %multiply_reduce_fusion = f32[]{:T(128)} fusion(f32[256,256]{1,0:T(8,128)} %get-tuple-element.16), kind=kLoop, calls=%fused_computation.2 | loop fusion | flops 131071 | bytes 262148 | tf_op jit(solution)/shard_map/reduce_sum | solution.py:224
  116.8 1.6 %multiply_reduce_fusion.1 = f32[]{:T(128)} fusion(f32[256,256]{1,0:T(8,128)} %get-tuple-element.15), kind=kLoop, calls=%fused_computation.4 | loop fusion | flops 131071 | bytes 262148 | tf_op jit(solution)/shard_map/reduce_sum | solution.py:223
  119.1 1.9 %multiply_bitcast_fusion = (f32[1,1,256,256]{3,2,1,0:T(8,128)}, f32[1,1,256,256]{3,2,1,0:T(8,128)}) fusion(f32[256,256]{1,0:T(8,128)} %get-tuple-element.16, f32[]{:T(128)S(6)} %rsqrt.7, f32[256,256]{1,0:T(8,128)} %get-tuple-element.15, f32[]{:T(128)S(6)} %rsqrt.6), kind=kLoop, calls=%fused_computation.1 | loop fusion | flops 131072 | bytes 1048584 | tf_op jit(solution)/shard_map/broadcast_in_dim | solution.py:225
  120.9 0.0 all-to-all-done
  120.9 1.0 convert_reduce_fusion
Async XLA Ops:
  7.2 13.5 %collective-permute-start = (bf16[1,1,256,256]{3,2,1,0:T(8,128)(2,1)}, bf16[1,1,256,256]{3,2,1,0:T(8,128)(2,1)S(1)}, u32[]{:S(2)}, u32[]{:S(2)}) collective-permute-start(bf16[1,1,256,256]{3,2,1,0:T(8,128)(2,1)} %param.9), channel_id=1, source_target_pairs={{0,16},{16,32},{32,48},{48,64},{64,80},{80,96},{96,112},{112,0},{1... | collective-permute-start | bytes 393224 | tf_op jit(solution)/shard_map/ppermute | solution.py:203
  8.9 11.7 %collective-permute-start.1 = (bf16[1,1,256,256]{3,2,1,0:T(8,128)(2,1)}, bf16[1,1,256,256]{3,2,1,0:T(8,128)(2,1)S(1)}, u32[]{:S(2)}, u32[]{:S(2)}) collective-permute-start(bf16[1,1,256,256]{3,2,1,0:T(8,128)(2,1)} %param.10), channel_id=1, source_target_pairs={{0,112},{16,0},{32,16},{48,32},{64,48},{80,64},{96,80},{112,96},{1... | collective-permute-start | bytes 393224 | tf_op jit(solution)/shard_map/ppermute | solution.py:203
  12.3 0.7 copy-start
  13.0 0.7 copy-start.1
  13.6 0.7 copy-start.2
  18.9 0.6 copy-start.3
  19.5 0.6 copy-start.4
  20.1 0.5 copy-start.5
  20.6 0.7 copy-start.6
  20.6 0.7 copy-start.7
  58.0 63.0 %all-to-all-start = ((bf16[16,256,256]{2,1,0:T(8,128)(2,1)}), bf16[16,256,256]{2,1,0:T(8,128)(2,1)S(1)}, u32[]{:S(2)}, u32[]{:S(2)}) async-start(bf16[16,256,256]{2,1,0:T(8,128)(2,1)} %convert_element_type.6), calls=%async_computation | async-start | bytes 4194304 | tf_op jit(solution)/shard_map/all_to_all | solution.py:220
  67.7 46.8 %all-reduce.3.cloned.1.call-start = ((), (), s32[]{:S(2)}) async-start(), calls=%async_computation.1 | async-start | bytes 1048576 | tf_op jit(solution)/shard_map/psum | solution.py:222
Sparse Core Ops, SparseCore 0:
  71.6 42.8 all-reduce.2

commit v2 on v1

v2 whole, which is shorter than its diff:
```python
import functools

import jax
import jax.numpy as jnp
from jax import lax
from jax.experimental import pallas as pl
from jax.experimental.pallas import tpu as pltpu
from jax.sharding import PartitionSpec as P

CHI = 256
UNITS = 50
OWNERS = 16
LANES = 128
TILE = 16
TILES = 32
CAP_TILES = 144
EMPTY = TILES - 1
GROUP = 10
STEPS = UNITS // GROUP
HALF = 128
PACKED = 2 * HALF + TILE
Z_CHIPS = 4
EPSILON = 1e-06
MESH = pl.DeviceIdType.MESH

F32 = jnp.float32
BF16 = jnp.bfloat16


def dot(x, y):
    return lax.dot_general(x, y, (((1,), (0,)), ((), ())), preferred_element_type=F32)


def dot_nt(x, y):
    return lax.dot_general(x, y, (((1,), (1,)), ((), ())), preferred_element_type=F32)


def dot_tn(x, y):
    return lax.dot_general(x, y, (((0,), (0,)), ((), ())), preferred_element_type=F32)


def iota(shape, axis):
    return lax.broadcasted_iota(jnp.int32, shape, axis)


def ones_where(mask):
    return jnp.where(mask, 1.0, 0.0).astype(BF16)


def plan_kernel(owner_ref, order_ref, size_ref, sector_ref, dest_ref, tile_ref):
    sector = sector_ref[...]
    named = jnp.zeros((1, LANES), F32)
    for s in range(OWNERS):
        named = jnp.where(sector == s, (owner_ref[s] + 1).astype(F32), named)
    up = iota((LANES, LANES), 0)
    across = iota((LANES, LANES), 1)
    before = ones_where(up < across)
    steps = ones_where(up == across) - ones_where(up + 1 == across)
    sizes = jnp.broadcast_to(size_ref[...].astype(F32), (8, LANES)).astype(BF16)
    starts = dot(sizes, before)[0:1]
    delta = dot(jnp.broadcast_to(named, (8, LANES)).astype(BF16), steps)[0:1]
    start_hi = jnp.floor((starts + 0.5) * (1.0 / LANES))
    start_lo = starts - LANES * start_hi
    place_hi = iota((104, LANES), 0).astype(F32)
    impulses = dot_nt(
        jnp.where(place_hi == start_hi, delta, 0.0).astype(BF16),
        ones_where(up.astype(F32) == start_lo),
    ).astype(BF16)
    inside = dot(impulses, ones_where(up <= across))
    totals = jnp.broadcast_to(inside[:, LANES - 1:LANES], (104, LANES)).astype(BF16)
    earlier = ones_where(iota((104, 104), 1) < iota((104, 104), 0))
    listed = inside + dot(earlier, totals)
    order = order_ref[...].astype(F32)
    bond = jnp.floor((order + 0.5) * (1.0 / UNITS))
    unit = order - UNITS * bond
    bonds = iota((CHI, LANES), 0).astype(F32)
    units = iota((64, LANES), 0).astype(F32)
    owned = jnp.zeros((64, CHI), F32)
    for first in range(0, 100, 10):
        left, right = [], []
        for h in range(first, first + 10):
            left.append(jnp.where(units == unit[h:h + 1], listed[h:h + 1], 0.0).astype(BF16))
            right.append(ones_where(bonds == bond[h:h + 1]))
        owned = owned + dot_nt(jnp.concatenate(left, axis=1), jnp.concatenate(right, axis=1))
    hits = [owned == float(o + 1) for o in range(OWNERS)]
    onehot = [ones_where(hit) for hit in hits]
    lower = ones_where(iota((CHI, CHI), 0) < iota((CHI, CHI), 1))
    offset = jnp.zeros((64, 1), F32)
    dest = jnp.full((64, CHI), -1.0, F32)
    lane = iota((64, LANES), 1)
    tile_counts = jnp.zeros((64, LANES), F32)
    tile_offsets = jnp.zeros((64, LANES), F32)
    for o in range(OWNERS):
        rank = dot(onehot[o], lower)
        amount = rank[:, CHI - 1:CHI] + onehot[o].astype(F32)[:, CHI - 1:CHI]
        tiles = jnp.floor((amount + (TILE - 1)) * (1.0 / TILE))
        dest = jnp.where(hits[o], TILE * offset + rank, dest)
        tile_counts = jnp.where(lane == o, tiles, tile_counts)
        tile_offsets = jnp.where(lane == o, offset, tile_offsets)
        offset = offset + tiles
    dest_ref[...] = dest
    eye = ones_where(iota((OWNERS, LANES), 0) == iota((OWNERS, LANES), 1))
    counts = dot_nt(eye, tile_counts.astype(BF16))
    offsets = dot_nt(eye, tile_offsets.astype(BF16))
    sofar = dot(counts.astype(BF16), ones_where(iota((64, 64), 0) < iota((64, 64), 1)))
    chunk = iota((OWNERS, 64), 1)
    base = offsets - sofar + (chunk * TILES).astype(F32)
    previous = jnp.where(chunk == 0, 0.0, pltpu.roll(base, 1, 1))
    jump = base - previous
    place = iota((OWNERS, CHI), 1).astype(F32)
    tile = place
    for u in range(UNITS):
        tile = tile + jnp.where(place >= sofar[:, u:u + 1], jump[:, u:u + 1], 0.0)
    used = sofar[:, UNITS - 1:UNITS] + counts[:, UNITS - 1:UNITS]
    tile_ref[...] = jnp.where(place < used, tile, float(EMPTY)).astype(jnp.int32)


def plan(sector_owner, row_order, block_size, block_sector):
    vmem = pl.BlockSpec(memory_space=pltpu.VMEM)
    return pl.pallas_call(
        plan_kernel,
        out_shape=(
            jax.ShapeDtypeStruct((64, CHI), F32),
            jax.ShapeDtypeStruct((OWNERS, CHI), jnp.int32),
        ),
        in_specs=[pl.BlockSpec(memory_space=pltpu.SMEM), vmem, vmem, vmem],
        out_specs=(vmem, vmem),
        cost_estimate=pl.CostEstimate(flops=2 * 64 * 12800 * 256, bytes_accessed=200000, transcendentals=0),
        compiler_params=pltpu.CompilerParams(vmem_limit_bytes=32 * 1024 * 1024),
    )(sector_owner, row_order, block_size, block_sector)


def sort_matrix(place):
    place = jnp.broadcast_to(place, (TILE, CHI))
    low = jnp.where(place < CHI, place, -1.0).astype(BF16)
    high = jnp.where(place >= CHI, place - CHI, -1.0).astype(BF16)
    rows = iota((CHI // TILE, TILE, CHI), 0) * TILE + iota((CHI // TILE, TILE, CHI), 1)
    rows = rows.astype(F32).astype(BF16)
    one, zero = jnp.ones((), BF16), jnp.zeros((), BF16)
    return jnp.concatenate(
        [jnp.where(rows == part[None], one, zero).reshape(CHI, CHI) for part in (low, high)], axis=0
    )


def pack(gram):
    upper, corner, lower = gram[:HALF, :HALF], gram[:HALF, HALF:], gram[HALF:, HALF:]
    row, col = iota((HALF, HALF), 0), iota((HALF, HALF), 1)
    diagonal = jnp.sum(jnp.where(row == col, lower, 0.0), axis=0, keepdims=True)
    return jnp.concatenate(
        [jnp.where(row <= col, upper, lower), corner, jnp.broadcast_to(diagonal, (TILE, HALF))], axis=0
    )


def unpack(packed):
    square, corner, diagonal = packed[:HALF], packed[HALF:CHI], packed[CHI:CHI + 1]
    row, col = iota((HALF, HALF), 0), iota((HALF, HALF), 1)
    turned = square.T
    upper = jnp.where(row <= col, square, turned)
    lower = jnp.where(row == col, diagonal, jnp.where(row > col, square, turned))
    return jnp.concatenate(
        [jnp.concatenate([upper, corner], axis=1), jnp.concatenate([corner.T, lower], axis=1)], axis=0
    )


def normalized(total):
    mean = jnp.sum(total * total, keepdims=True) * (1.0 / (CHI * CHI))
    return total * lax.rsqrt(mean + EPSILON)


def column_kernel(
    tile_ref, dest_ref, left_ref, right_ref, edge_hbm, proj_left_hbm, proj_right_hbm,
    out_left, out_right, out_gram,
    edge, proj_left, proj_right, enlarged, wide, sorted_rows, listed,
    left_sum, right_sum, left_other, right_other,
    mine, to_mate, from_mate, to_row, from_row, to_sec, from_sec,
    load_sem, corner_send, corner_recv, mate_send, mate_recv, row_send, row_recv, sec_send, sec_recv,
):
    row, sec = lax.axis_index("row"), lax.axis_index("sec")
    z, core = row // 2, row % 2
    mate = {"row": z * 2 + (1 - core)}
    partner = {"sec": 1 - sec}
    ahead = [{"row": ((z + dz) % Z_CHIPS) * 2 + core} for dz in range(1, Z_CHIPS)]

    barrier = pltpu.get_barrier_semaphore()
    for other in [mate, partner] + ahead:
        pl.semaphore_signal(barrier, inc=1, device_id=other, device_id_type=MESH)

    pairs = ((edge_hbm, edge), (proj_left_hbm, proj_left), (proj_right_hbm, proj_right))

    def load(k, i):
        part = pl.ds(i * GROUP, GROUP)
        return pltpu.make_async_copy(pairs[k][0].at[part], pairs[k][1].at[part], load_sem.at[k, i])

    for i in range(STEPS):
        load(0, i).start()
        load(1, i).start()
    for i in range(STEPS):
        load(2, i).start()

    left_sum[...] = jnp.zeros_like(left_sum)
    right_sum[...] = jnp.zeros_like(right_sum)

    @pl.loop(0, STEPS)
    def _(i):
        load(0, i).wait()
        load(1, i).wait()
        for j in range(GROUP):
            enlarged[pl.ds(j * CHI, CHI), :] = dot(left_ref[...], edge[i * GROUP + j]).astype(BF16)
        chunk = proj_left[pl.ds(i * GROUP, GROUP)].reshape(GROUP * CHI, CHI)
        left_sum[...] += dot_tn(chunk, enlarged[...])
        for j in range(GROUP):
            u = i * GROUP + j
            ordered = dot(sort_matrix(dest_ref[pl.ds(u, 1), :]), enlarged[pl.ds(j * CHI, CHI), :])
            sorted_rows[pl.ds(u * TILES, TILES)] = ordered.astype(BF16).reshape(TILES, TILE, CHI)

    pl.semaphore_wait(barrier, 2 + len(ahead))

    def corner_copy(k):
        source, target = ((left_sum, left_other), (right_sum, right_other))[k]
        return pltpu.make_async_remote_copy(
            src_ref=source, dst_ref=target, send_sem=corner_send.at[k], recv_sem=corner_recv.at[k],
            device_id=partner, device_id_type=MESH,
        )

    corner_copy(0).start()

    @pl.loop(0, STEPS)
    def _(i):
        load(2, i).wait()
        for j in range(GROUP):
            wide[:, pl.ds(j * CHI, CHI)] = dot(edge[i * GROUP + j], right_ref[...]).astype(BF16)
        chunk = proj_right[pl.ds(i * GROUP, GROUP)].reshape(GROUP * CHI, CHI)
        right_sum[...] += dot(wide[...], chunk)

    corner_copy(1).start()

    def owner_gram(k, owner):
        for t in range(CAP_TILES):
            listed[k, pl.ds(t * TILE, TILE), :] = sorted_rows[tile_ref[owner, t]]
        rows = listed[k]
        return pack(dot_tn(rows, rows))

    def mate_copy(i):
        return pltpu.make_async_remote_copy(
            src_ref=to_mate.at[i], dst_ref=from_mate.at[i], send_sem=mate_send.at[i], recv_sem=mate_recv.at[i],
            device_id=mate, device_id_type=MESH,
        )

    def row_copy(j):
        target = {"row": ((z + 1 + j // 2) % Z_CHIPS) * 2 + core}
        return pltpu.make_async_remote_copy(
            src_ref=to_row.at[j], dst_ref=from_row.at[j], send_sem=row_send.at[j], recv_sem=row_recv.at[j],
            device_id=target, device_id_type=MESH,
        )

    sec_copy = pltpu.make_async_remote_copy(
        src_ref=to_sec, dst_ref=from_sec, send_sem=sec_send, recv_sem=sec_recv,
        device_id=partner, device_id_type=MESH,
    )

    @pl.loop(0, 2 * Z_CHIPS)
    def _(i):
        z_owner = (z + 1 + i // 2) % Z_CHIPS
        sec_owner = (sec + 1 + i) % 2
        to_mate[i] = owner_gram(0, z_owner * 4 + (1 - core) * 2 + sec_owner)
        mate_copy(i).start()
        mine[i] = owner_gram(1, z_owner * 4 + core * 2 + sec_owner)

        @pl.when((i >= 1) & (i <= 6))
        def _():
            mate_copy(i - 1).wait_recv()
            to_row[i - 1] = (mine[i - 1] + from_mate[i - 1]).astype(BF16)
            row_copy(i - 1).start()

    def column_sum(r):
        mate_copy(6 + r).wait_recv()
        total = mine[6 + r] + from_mate[6 + r]
        for k in range(Z_CHIPS - 1):
            row_copy(2 * k + r).wait_recv()
            total = total + from_row[2 * k + r].astype(F32)
        return total

    to_sec[...] = column_sum(0).astype(BF16)
    sec_copy.start()
    corner_copy(0).wait()
    out_left[...] = normalized(left_sum[...] + left_other[...])
    corner_copy(1).wait()
    out_right[...] = normalized(right_sum[...] + right_other[...])
    total = column_sum(1)
    sec_copy.wait_recv()
    out_gram[...] = unpack(total + from_sec[...].astype(F32))
    for i in range(2 * Z_CHIPS):
        mate_copy(i).wait_send()
    for j in range(2 * (Z_CHIPS - 1)):
        row_copy(j).wait_send()
    sec_copy.wait_send()


def column(tiles, dest, from_left, from_right, edge, proj_left, proj_right):
    vmem = pl.BlockSpec(memory_space=pltpu.VMEM)
    anywhere = pl.BlockSpec(memory_space=pl.ANY)
    square = jax.ShapeDtypeStruct((CHI, CHI), F32)
    whole = pltpu.VMEM((UNITS, CHI, CHI), BF16)
    dma = pltpu.SemaphoreType.DMA
    return pl.pallas_call(
        column_kernel,
        in_specs=[pl.BlockSpec(memory_space=pltpu.SMEM), vmem, vmem, vmem, anywhere, anywhere, anywhere],
        out_specs=(vmem, vmem, vmem),
        out_shape=(square, square, square),
        scratch_shapes=[
            whole, whole, whole,
            pltpu.VMEM((GROUP * CHI, CHI), BF16),
            pltpu.VMEM((CHI, GROUP * CHI), BF16),
            pltpu.VMEM((UNITS * TILES, TILE, CHI), BF16),
            pltpu.VMEM((2, CAP_TILES * TILE, CHI), BF16),
            pltpu.VMEM((CHI, CHI), F32), pltpu.VMEM((CHI, CHI), F32),
            pltpu.VMEM((CHI, CHI), F32), pltpu.VMEM((CHI, CHI), F32),
            pltpu.VMEM((8, PACKED, HALF), F32),
            pltpu.VMEM((8, PACKED, HALF), F32),
            pltpu.VMEM((8, PACKED, HALF), F32),
            pltpu.VMEM((6, PACKED, HALF), BF16),
            pltpu.VMEM((6, PACKED, HALF), BF16),
            pltpu.VMEM((PACKED, HALF), BF16),
            pltpu.VMEM((PACKED, HALF), BF16),
            dma((3, STEPS)), dma((2,)), dma((2,)), dma((8,)), dma((8,)), dma((6,)), dma((6,)), dma, dma,
        ],
        cost_estimate=pl.CostEstimate(flops=9 * 2 * 12800 * 65536, bytes_accessed=24 << 20, transcendentals=0),
        compiler_params=pltpu.CompilerParams(
            collective_id=0, has_side_effects=True, vmem_limit_bytes=60 * 1024 * 1024
        ),
    )(tiles, dest, from_left, from_right, edge, proj_left, proj_right)


def from_behind(value, axis, steps):
    count = lax.axis_size(axis)
    pairs = [(source, (source + steps) % count) for source in range(count)]
    return lax.ppermute(value, axis, pairs)


def body(
    corner_left, corner_right, edge_top, proj_left, proj_right, row_order, block_size, block_sector, sector_owner,
):
    from_left = from_behind(corner_left, "col", 1)[0, 0]
    from_right = from_behind(corner_right, "col", -1)[0, 0]
    dest, tiles = plan(
        sector_owner,
        row_order.reshape(100, LANES),
        block_size.reshape(1, LANES),
        block_sector.reshape(1, LANES),
    )
    edge = jnp.transpose(edge_top[0, 0], (1, 0, 2))
    left = jnp.transpose(proj_left[0, 0], (1, 0, 2))
    new_left, new_right, sector_gram = column(tiles, dest, from_left, from_right, edge, left, proj_right[0, 0])
    return (new_left[None, None], new_right[None, None], sector_gram[None, None])


def solution(mesh):
    in_specs = (
        P("col", "row", None, None),
        P("col", "row", None, None),
        P("col", "row", None, "sec", None),
        P("col", "row", None, "sec", None),
        P("col", "row", "sec", None, None),
        P("col", "row", "sec", None),
        P("col", "row", "sec", None),
        P("col", "row", "sec", None, None),
        P(),
    )
    out_specs = (
        P("col", "row", None, None),
        P("col", "row", None, None),
        P("col", ("row", "sec"), None, None),
    )
    return jax.shard_map(body, mesh=mesh, in_specs=in_specs, out_specs=out_specs, check_vma=False)
```

time: 130 us -> 57.3 us (0.44)
  waiting for transfers between devices: 46.7 us -> 0.01 us
  between operations: 15.5 us -> 0.68 us
  other arithmetic: 10.8 us -> 0.93 us
  starting transfers between devices: 14 us -> 4.2 us
  local copies, waits for them, and re-layouts: 4.37 us -> 8.88 us
  Pallas kernels: 37.5 us -> 41.8 us
    psum x1 -> x0, waiting for transfers between devices: 46 us -> none  [body(): left_sum, right_sum = lax.psum((left_part, right_part), 'sec')]
    all_to_all x1 -> x0, starting transfers between devices: 9.71 us -> none  [body(): lax.all_to_all(grams.astype(BF16), ('row', 'sec'), split_axis=0, concat_a...]
    unnamed x16 -> x17, local copies, waits for them, and re-layouts: 4.37 us -> 8.88 us
    reduce_sum x3 -> x0, other arithmetic: 4.23 us -> none  [the longest x1 1.62 us: body(): new_left = left_sum * lax.rsqrt(jnp.mean(left_sum * left_sum) + EPSILON)]
    pallas_call x1, Pallas kernels: 32.9 us -> 36.7 us  [column(): pl.pallas_call(column_kernel, in_specs=[pl.BlockSpec(memory_space=pltpu.S...]
    convert_element_type x1 -> x0, other arithmetic: 3.77 us -> none  [body(): grams.astype(BF16)]
    broadcast_in_dim x1 -> x0, other arithmetic: 1.86 us -> none  [body(): return (new_left[None, None], new_right[None, None], sector_gram)]
  transfers between devices with their start and end apart: 4 -> 2, of which waited for: 1 -> 0; matrix products, arithmetic and copies ran while one was open for 5% -> 2% of each run, Pallas kernels for 4% -> 9%
where the time goes in v2:
time: 57.3 us; the launch traced here: 56.5 us
  Pallas kernels  41.8 us (73%)
  local copies, waits for them, and re-layouts  8.88 us (15%)
  starting transfers between devices  4.2 us (7%)
  other arithmetic  0.93 us (2%)
  between operations  0.68 us (1%)
    pallas_call x1, Pallas kernels, column(): pl.pallas_call(column_kernel, in_specs=[pl.BlockSpec(memory_space=pltpu.S...  36.7 us
    unnamed x17, local copies, waits for them, and re-layouts  8.88 us
    pallas_call x1, Pallas kernels, plan(): pl.pallas_call(plan_kernel, out_shape=(jax.ShapeDtypeStruct((64, CHI), F3...  5.07 us
    ppermute x2, starting transfers between devices, from_behind(): return lax.ppermute(value, axis, pairs)  4.2 us
  transfers between devices with their start and end apart: 2, of which 0 were waited for; matrix products, arithmetic and copies ran while one was open for 2% of the time, Pallas kernels for 9%

profile of v2, /device:TPU:0, one launch (start us, length us, event | category | flops | bytes accessed | tf_op | source)
XLA Modules:
  0.0 56.5 jit_solution(9352960483244197051)
XLA Ops:
  0.6 1.7 %collective-permute-start = (bf16[1,1,256,256]{3,2,1,0:T(8,128)(2,1)}, bf16[1,1,256,256]{3,2,1,0:T(8,128)(2,1)S(1)}, u32[]{:S(2)}, u32[]{:S(2)}) collective-permute-start(bf16[1,1,256,256]{3,2,1,0:T(8,128)(2,1)} %param.9), channel_id=1, source_target_pairs={{0,16},{16,32},{32,48},{48,64},{64,80},{80,96},{96,112},{112,0},{1... | collective-permute-start | bytes 393224 | tf_op jit(solution)/shard_map/ppermute | solution.py:337
  2.4 2.5 %collective-permute-start.1 = (bf16[1,1,256,256]{3,2,1,0:T(8,128)(2,1)}, bf16[1,1,256,256]{3,2,1,0:T(8,128)(2,1)S(1)}, u32[]{:S(2)}, u32[]{:S(2)}) collective-permute-start(bf16[1,1,256,256]{3,2,1,0:T(8,128)(2,1)} %param.10), channel_id=1, source_target_pairs={{0,112},{16,0},{32,16},{48,32},{64,48},{80,64},{96,80},{112,96},{1... | collective-permute-start | bytes 393224 | tf_op jit(solution)/shard_map/ppermute | solution.py:337
  4.8 0.9 %reduce = s32[12800]{0:T(1024)S(1)} reduce(s32[1,1,1,12800]{3,2,1,0:T(1,128)} %param.14, s32[]{:T(128)} %constant.8), dimensions={0,1,2}, to_apply=%param.14.reduce_sub_computation | reduce | bytes 102404 | tf_op args[5]
  5.8 0.0 copy-start
  5.8 0.6 %copy-done = s32[16]{0:T(128)S(1)} copy-done((s32[16]{0:T(128)S(1)}, s32[16]{0:T(128)}, u32[]{:S(2)}) %copy-start) | copy-done | bytes 88
  6.4 0.0 copy-start.1
  6.4 0.7 %copy-done.1 = s32[1,1,1,128]{3,2,1,0:T(1,128)S(1)} copy-done((s32[1,1,1,128]{3,2,1,0:T(1,128)S(1)}, s32[1,1,1,128]{3,2,1,0:T(1,128)}, u32[]{:S(2)}) %copy-start.1) | copy-done | bytes 536
  7.1 0.0 copy-start.2
  7.1 0.7 %copy-done.2 = s32[1,1,1,128,1]{3,4,2,1,0:T(1,128)S(1)} copy-done((s32[1,1,1,128,1]{3,4,2,1,0:T(1,128)S(1)}, s32[1,1,1,128,1]{3,4,2,1,0:T(1,128)}, u32[]{:S(2)}) %copy-start.2) | copy-done | bytes 536
  7.7 5.1 %shard_map.112 = (f32[64,256]{1,0:T(8,128)S(1)}, s32[16,256]{1,0:T(8,128)S(1)}) custom-call(s32[16]{0:T(128)S(1)} %copy-done, s32[100,128]{1,0:T(8,128)S(1)} %bitcast.15, s32[1,128]{1,0:T(1,128)S(1)} %bitcast.16, s32[1,128]{1,0:T(1,128)S(1)} %bitcast.17), custom_call_target="tpu_custom_call" | custom-call | flops 419430400 | bytes 200000 | tf_op jit(solution)/shard_map/pallas_call | solution.py:120
  12.8 0.0 copy-start.3
  12.8 0.6 %copy-done.3 = f32[64,256]{1,0:T(8,128)} copy-done((f32[64,256]{1,0:T(8,128)}, f32[64,256]{1,0:T(8,128)S(1)}, u32[]{:S(2)}) %copy-start.3) | copy-done | bytes 65560
  13.4 0.0 copy-start.4
  13.4 0.6 %copy-done.4 = s32[16,256]{1,0:T(8,128)} copy-done((s32[16,256]{1,0:T(8,128)}, s32[16,256]{1,0:T(8,128)S(1)}, u32[]{:S(2)}) %copy-start.4) | copy-done | bytes 16408
  14.0 0.0 collective-permute-done
  14.0 0.0 copy-start.5
  14.0 0.0 collective-permute-done.1
  14.1 0.0 copy-start.6
  14.1 0.6 %copy-done.5 = bf16[1,1,256,256]{3,2,1,0:T(8,128)(2,1)} copy-done((bf16[1,1,256,256]{3,2,1,0:T(8,128)(2,1)}, bf16[1,1,256,256]{3,2,1,0:T(8,128)(2,1)S(1)}, u32[]{:S(2)}) %copy-start.5) | copy-done | bytes 131096
  14.7 0.0 copy-done.6
  14.7 36.7 %shard_map.113 = (f32[256,256]{1,0:T(8,128)}, f32[256,256]{1,0:T(8,128)}, f32[256,256]{1,0:T(8,128)}) custom-call(s32[16,256]{1,0:T(8,128)} %copy-done.4, f32[64,256]{1,0:T(8,128)} %copy-done.3, bf16[256,256]{1,0:T(8,128)(2,1)} %bitcast.24, bf16[256,256]{1,0:T(8,128)(2,1)} %bitcast.25, bf16[50,256,256]{2,1,0:T(8,128)(2,1)} %bitcast.21, ...), custom_call_target="tpu_custom_call" | custom-call | flops 15099494400 | bytes 25165824 | tf_op jit(solution)/shard_map/pallas_call | solution.py:305
  51.5 1.7 %copy.15 = f32[1,1,256,256]{3,2,1,0:T(8,128)} copy(f32[1,1,256,256]{3,2,1,0:T(8,128)} %bitcast.20) | data formatting | bytes 524288
  53.1 1.7 %copy.16 = f32[1,1,256,256]{3,2,1,0:T(8,128)} copy(f32[1,1,256,256]{3,2,1,0:T(8,128)} %bitcast.19) | data formatting | bytes 524288
  54.8 1.7 %copy.17 = f32[1,1,256,256]{3,2,1,0:T(8,128)} copy(f32[1,1,256,256]{3,2,1,0:T(8,128)} %bitcast.18) | data formatting | bytes 524288
Async XLA Ops:
  0.6 13.4 %collective-permute-start = (bf16[1,1,256,256]{3,2,1,0:T(8,128)(2,1)}, bf16[1,1,256,256]{3,2,1,0:T(8,128)(2,1)S(1)}, u32[]{:S(2)}, u32[]{:S(2)}) collective-permute-start(bf16[1,1,256,256]{3,2,1,0:T(8,128)(2,1)} %param.9), channel_id=1, source_target_pairs={{0,16},{16,32},{32,48},{48,64},{64,80},{80,96},{96,112},{112,0},{1... | collective-permute-start | bytes 393224 | tf_op jit(solution)/shard_map/ppermute | solution.py:337
  2.4 11.7 %collective-permute-start.1 = (bf16[1,1,256,256]{3,2,1,0:T(8,128)(2,1)}, bf16[1,1,256,256]{3,2,1,0:T(8,128)(2,1)S(1)}, u32[]{:S(2)}, u32[]{:S(2)}) collective-permute-start(bf16[1,1,256,256]{3,2,1,0:T(8,128)(2,1)} %param.10), channel_id=1, source_target_pairs={{0,112},{16,0},{32,16},{48,32},{64,48},{80,64},{96,80},{112,96},{1... | collective-permute-start | bytes 393224 | tf_op jit(solution)/shard_map/ppermute | solution.py:337
  5.8 0.7 %copy-start = (s32[16]{0:T(128)S(1)}, s32[16]{0:T(128)}, u32[]{:S(2)}) copy-start(s32[16]{0:T(128)} %owner_ref.1) | copy-start | bytes 196
  6.4 0.7 %copy-start.1 = (s32[1,1,1,128]{3,2,1,0:T(1,128)S(1)}, s32[1,1,1,128]{3,2,1,0:T(1,128)}, u32[]{:S(2)}) copy-start(s32[1,1,1,128]{3,2,1,0:T(1,128)} %param.15) | copy-start | bytes 1540
  7.1 0.7 %copy-start.2 = (s32[1,1,1,128,1]{3,4,2,1,0:T(1,128)S(1)}, s32[1,1,1,128,1]{3,4,2,1,0:T(1,128)}, u32[]{:S(2)}) copy-start(s32[1,1,1,128,1]{3,4,2,1,0:T(1,128)} %param.16) | copy-start | bytes 1540
  12.8 0.6 %copy-start.3 = (f32[64,256]{1,0:T(8,128)}, f32[64,256]{1,0:T(8,128)S(1)}, u32[]{:S(2)}) copy-start(f32[64,256]{1,0:T(8,128)S(1)} %get-tuple-element.9.dest_ref) | copy-start | bytes 196612
  13.4 0.6 %copy-start.4 = (s32[16,256]{1,0:T(8,128)}, s32[16,256]{1,0:T(8,128)S(1)}, u32[]{:S(2)}) copy-start(s32[16,256]{1,0:T(8,128)S(1)} %get-tuple-element.8.tile_ref) | copy-start | bytes 49156
  14.0 0.7 %copy-start.5 = (bf16[1,1,256,256]{3,2,1,0:T(8,128)(2,1)}, bf16[1,1,256,256]{3,2,1,0:T(8,128)(2,1)S(1)}, u32[]{:S(2)}) copy-start(bf16[1,1,256,256]{3,2,1,0:T(8,128)(2,1)S(1)} %collective-permute-done) | copy-start | bytes 393220
  14.1 0.7 %copy-start.6 = (bf16[1,1,256,256]{3,2,1,0:T(8,128)(2,1)}, bf16[1,1,256,256]{3,2,1,0:T(8,128)(2,1)S(1)}, u32[]{:S(2)}) copy-start(bf16[1,1,256,256]{3,2,1,0:T(8,128)(2,1)S(1)} %collective-permute-done.1) | copy-start | bytes 393220

commit v3 on v2

--- a/solution.py
+++ b/solution.py
@@ -47,54 +47,60 @@
     return jnp.where(mask, 1.0, 0.0).astype(BF16)
 
 
-def plan_kernel(owner_ref, order_ref, size_ref, sector_ref, dest_ref, tile_ref):
+def find_owners(owner_ref, order_ref, size_ref, sector_ref):
     sector = sector_ref[...]
     named = jnp.zeros((1, LANES), F32)
     for s in range(OWNERS):
         named = jnp.where(sector == s, (owner_ref[s] + 1).astype(F32), named)
     up = iota((LANES, LANES), 0)
     across = iota((LANES, LANES), 1)
-    before = ones_where(up < across)
     steps = ones_where(up == across) - ones_where(up + 1 == across)
-    sizes = jnp.broadcast_to(size_ref[...].astype(F32), (8, LANES)).astype(BF16)
-    starts = dot(sizes, before)[0:1]
-    delta = dot(jnp.broadcast_to(named, (8, LANES)).astype(BF16), steps)[0:1]
+    sizes = jnp.broadcast_to(size_ref[...].astype(F32), (TILE, LANES)).astype(BF16)
+    starts = dot(sizes, ones_where(up < across))[0:1]
+    delta = dot(jnp.broadcast_to(named, (TILE, LANES)).astype(BF16), steps)[0:1]
     start_hi = jnp.floor((starts + 0.5) * (1.0 / LANES))
     start_lo = starts - LANES * start_hi
-    place_hi = iota((104, LANES), 0).astype(F32)
+    place_hi = iota((112, LANES), 0).astype(F32)
     impulses = dot_nt(
         jnp.where(place_hi == start_hi, delta, 0.0).astype(BF16),
         ones_where(up.astype(F32) == start_lo),
     ).astype(BF16)
     inside = dot(impulses, ones_where(up <= across))
-    totals = jnp.broadcast_to(inside[:, LANES - 1:LANES], (104, LANES)).astype(BF16)
-    earlier = ones_where(iota((104, 104), 1) < iota((104, 104), 0))
-    listed = inside + dot(earlier, totals)
-    order = order_ref[...].astype(F32)
-    bond = jnp.floor((order + 0.5) * (1.0 / UNITS))
-    unit = order - UNITS * bond
-    bonds = iota((CHI, LANES), 0).astype(F32)
-    units = iota((64, LANES), 0).astype(F32)
+    totals = jnp.broadcast_to(inside[:, LANES - 1:LANES], (112, LANES)).astype(BF16)
+    listed = inside + dot(ones_where(iota((112, 112), 1) < iota((112, 112), 0)), totals)
+    bonds = (iota((CHI // TILE, TILE, LANES), 0) * TILE + iota((CHI // TILE, TILE, LANES), 1)).astype(F32).astype(BF16)
+    units = (iota((4, TILE, LANES), 0) * TILE + iota((4, TILE, LANES), 1)).astype(F32).astype(BF16)
+    one, zero = jnp.ones((), BF16), jnp.zeros((), BF16)
     owned = jnp.zeros((64, CHI), F32)
-    for first in range(0, 100, 10):
+    for first in range(0, 100, 20):
         left, right = [], []
-        for h in range(first, first + 10):
-            left.append(jnp.where(units == unit[h:h + 1], listed[h:h + 1], 0.0).astype(BF16))
-            right.append(ones_where(bonds == bond[h:h + 1]))
+        for h in range(first, first + 20):
+            order = order_ref[:, h * LANES:(h + 1) * LANES].astype(F32)
+            bond = jnp.floor((order + 0.5) * (1.0 / UNITS))
+            unit = order - UNITS * bond
+            bond, unit, name = (
+                jnp.broadcast_to(x, (TILE, LANES)).astype(BF16)[None] for x in (bond, unit, listed[h:h + 1])
+            )
+            left.append(jnp.where(units == unit, name, zero).reshape(64, LANES))
+            right.append(jnp.where(bonds == bond, one, zero).reshape(CHI, LANES))
         owned = owned + dot_nt(jnp.concatenate(left, axis=1), jnp.concatenate(right, axis=1))
+    return owned
+
+
+def plan(owner_ref, order_ref, size_ref, sector_ref, dest_ref, tile_ref):
+    owned = find_owners(owner_ref, order_ref, size_ref, sector_ref)
     hits = [owned == float(o + 1) for o in range(OWNERS)]
     onehot = [ones_where(hit) for hit in hits]
-    lower = ones_where(iota((CHI, CHI), 0) < iota((CHI, CHI), 1))
+    ranks = dot(jnp.concatenate(onehot, axis=0), ones_where(iota((CHI, CHI), 0) <= iota((CHI, CHI), 1)))
     offset = jnp.zeros((64, 1), F32)
     dest = jnp.full((64, CHI), -1.0, F32)
     lane = iota((64, LANES), 1)
     tile_counts = jnp.zeros((64, LANES), F32)
     tile_offsets = jnp.zeros((64, LANES), F32)
     for o in range(OWNERS):
-        rank = dot(onehot[o], lower)
-        amount = rank[:, CHI - 1:CHI] + onehot[o].astype(F32)[:, CHI - 1:CHI]
-        tiles = jnp.floor((amount + (TILE - 1)) * (1.0 / TILE))
-        dest = jnp.where(hits[o], TILE * offset + rank, dest)
+        rank = ranks[o * 64:(o + 1) * 64]
+        tiles = jnp.floor((rank[:, CHI - 1:CHI] + (TILE - 1)) * (1.0 / TILE))
+        dest = jnp.where(hits[o], (TILE * offset - 1.0) + rank, dest)
         tile_counts = jnp.where(lane == o, tiles, tile_counts)
         tile_offsets = jnp.where(lane == o, offset, tile_offsets)
         offset = offset + tiles
@@ -115,21 +121,6 @@
     tile_ref[...] = jnp.where(place < used, tile, float(EMPTY)).astype(jnp.int32)
 
 
-def plan(sector_owner, row_order, block_size, block_sector):
-    vmem = pl.BlockSpec(memory_space=pltpu.VMEM)
-    return pl.pallas_call(
-        plan_kernel,
-        out_shape=(
-            jax.ShapeDtypeStruct((64, CHI), F32),
-            jax.ShapeDtypeStruct((OWNERS, CHI), jnp.int32),
-        ),
-        in_specs=[pl.BlockSpec(memory_space=pltpu.SMEM), vmem, vmem, vmem],
-        out_specs=(vmem, vmem),
-        cost_estimate=pl.CostEstimate(flops=2 * 64 * 12800 * 256, bytes_accessed=200000, transcendentals=0),
-        compiler_params=pltpu.CompilerParams(vmem_limit_bytes=32 * 1024 * 1024),
-    )(sector_owner, row_order, block_size, block_sector)
-
-
 def sort_matrix(place):
     place = jnp.broadcast_to(place, (TILE, CHI))
     low = jnp.where(place < CHI, place, -1.0).astype(BF16)
@@ -168,21 +159,25 @@
 
 
 def column_kernel(
-    tile_ref, dest_ref, left_ref, right_ref, edge_hbm, proj_left_hbm, proj_right_hbm,
+    owner_ref, order_hbm, size_hbm, sector_hbm, left_hbm, right_hbm, edge_hbm, proj_left_hbm, proj_right_hbm,
     out_left, out_right, out_gram,
+    order, sizes, sectors, dest, tile_plan, tile_list, from_left, from_right,
     edge, proj_left, proj_right, enlarged, wide, sorted_rows, listed,
     left_sum, right_sum, left_other, right_other,
-    mine, to_mate, from_mate, to_row, from_row, to_sec, from_sec,
-    load_sem, corner_send, corner_recv, mate_send, mate_recv, row_send, row_recv, sec_send, sec_recv,
+    gram_sum, mine, to_mate, from_mate, to_row, from_row, to_sec, from_sec,
+    list_sem, tile_sem, shift_send, shift_recv, load_sem, corner_send, corner_recv, mate_send, mate_recv, row_send, row_recv, sec_send, sec_recv, result_sem,
 ):
-    row, sec = lax.axis_index("row"), lax.axis_index("sec")
+    col, row, sec = lax.axis_index("col"), lax.axis_index("row"), lax.axis_index("sec")
     z, core = row // 2, row % 2
     mate = {"row": z * 2 + (1 - core)}
     partner = {"sec": 1 - sec}
     ahead = [{"row": ((z + dz) % Z_CHIPS) * 2 + core} for dz in range(1, Z_CHIPS)]
 
+    sides = [{"col": (col + 1) % 8}, {"col": (col + 7) % 8}]
+    others = [mate, partner] + ahead + sides
+
     barrier = pltpu.get_barrier_semaphore()
-    for other in [mate, partner] + ahead:
+    for other in others:
         pl.semaphore_signal(barrier, inc=1, device_id=other, device_id_type=MESH)
 
     pairs = ((edge_hbm, edge), (proj_left_hbm, proj_left), (proj_right_hbm, proj_right))
@@ -191,12 +186,35 @@
         part = pl.ds(i * GROUP, GROUP)
         return pltpu.make_async_copy(pairs[k][0].at[part], pairs[k][1].at[part], load_sem.at[k, i])
 
+    lists = [
+        pltpu.make_async_copy(source, target, list_sem.at[k])
+        for k, (source, target) in enumerate(((order_hbm, order), (size_hbm, sizes), (sector_hbm, sectors)))
+    ]
+    for copy in lists:
+        copy.start()
     for i in range(STEPS):
         load(0, i).start()
         load(1, i).start()
     for i in range(STEPS):
         load(2, i).start()
 
+    pl.semaphore_wait(barrier, len(others))
+    shifts = [
+        pltpu.make_async_remote_copy(
+            src_ref=source, dst_ref=target, send_sem=shift_send.at[k], recv_sem=shift_recv.at[k],
+            device_id=sides[k], device_id_type=MESH,
+        )
+        for k, (source, target) in enumerate(((left_hbm, from_left), (right_hbm, from_right)))
+    ]
+    for copy in shifts:
+        copy.start()
+    for copy in lists:
+        copy.wait()
+    plan(owner_ref, order, sizes, sectors, dest, tile_plan)
+    tile_copy = pltpu.make_async_copy(tile_plan, tile_list, tile_sem)
+    tile_copy.start()
+    shifts[0].wait()
+
     left_sum[...] = jnp.zeros_like(left_sum)
     right_sum[...] = jnp.zeros_like(right_sum)
 
@@ -205,15 +223,13 @@
         load(0, i).wait()
         load(1, i).wait()
         for j in range(GROUP):
-            enlarged[pl.ds(j * CHI, CHI), :] = dot(left_ref[...], edge[i * GROUP + j]).astype(BF16)
+            enlarged[pl.ds(j * CHI, CHI), :] = dot(from_left[...], edge[i * GROUP + j]).astype(BF16)
         chunk = proj_left[pl.ds(i * GROUP, GROUP)].reshape(GROUP * CHI, CHI)
         left_sum[...] += dot_tn(chunk, enlarged[...])
         for j in range(GROUP):
             u = i * GROUP + j
-            ordered = dot(sort_matrix(dest_ref[pl.ds(u, 1), :]), enlarged[pl.ds(j * CHI, CHI), :])
+            ordered = dot(sort_matrix(dest[pl.ds(u, 1), :]), enlarged[pl.ds(j * CHI, CHI), :])
             sorted_rows[pl.ds(u * TILES, TILES)] = ordered.astype(BF16).reshape(TILES, TILE, CHI)
-
-    pl.semaphore_wait(barrier, 2 + len(ahead))
 
     def corner_copy(k):
         source, target = ((left_sum, left_other), (right_sum, right_other))[k]
@@ -223,20 +239,27 @@
         )
 
     corner_copy(0).start()
+    shifts[1].wait()
 
     @pl.loop(0, STEPS)
     def _(i):
         load(2, i).wait()
         for j in range(GROUP):
-            wide[:, pl.ds(j * CHI, CHI)] = dot(edge[i * GROUP + j], right_ref[...]).astype(BF16)
+            wide[:, pl.ds(j * CHI, CHI)] = dot(edge[i * GROUP + j], from_right[...]).astype(BF16)
         chunk = proj_right[pl.ds(i * GROUP, GROUP)].reshape(GROUP * CHI, CHI)
         right_sum[...] += dot(wide[...], chunk)
 
     corner_copy(1).start()
+    tile_copy.wait()
+
+    def result(k):
+        source, target = ((left_sum, out_left), (right_sum, out_right), (gram_sum, out_gram))[k]
+        return pltpu.make_async_copy(source, target, result_sem.at[k])
 
     def owner_gram(k, owner):
         for t in range(CAP_TILES):
-            listed[k, pl.ds(t * TILE, TILE), :] = sorted_rows[tile_ref[owner, t]]
+            tile = jnp.minimum(jnp.maximum(tile_list[owner, t], 0), UNITS * TILES - 1)
+            listed[k, pl.ds(t * TILE, TILE), :] = sorted_rows[tile]
         rows = listed[k]
         return pack(dot_tn(rows, rows))
 
@@ -283,31 +306,43 @@
     to_sec[...] = column_sum(0).astype(BF16)
     sec_copy.start()
     corner_copy(0).wait()
-    out_left[...] = normalized(left_sum[...] + left_other[...])
+    left_sum[...] = normalized(left_sum[...] + left_other[...])
+    result(0).start()
     corner_copy(1).wait()
-    out_right[...] = normalized(right_sum[...] + right_other[...])
+    right_sum[...] = normalized(right_sum[...] + right_other[...])
+    result(1).start()
     total = column_sum(1)
     sec_copy.wait_recv()
-    out_gram[...] = unpack(total + from_sec[...].astype(F32))
+    gram_sum[...] = unpack(total + from_sec[...].astype(F32))
+    result(2).start()
     for i in range(2 * Z_CHIPS):
         mate_copy(i).wait_send()
     for j in range(2 * (Z_CHIPS - 1)):
         row_copy(j).wait_send()
     sec_copy.wait_send()
-
-
-def column(tiles, dest, from_left, from_right, edge, proj_left, proj_right):
-    vmem = pl.BlockSpec(memory_space=pltpu.VMEM)
-    anywhere = pl.BlockSpec(memory_space=pl.ANY)
+    for k in range(3):
+        result(k).wait()
+
+
+def column(sector_owner, row_order, block_size, block_sector, corner_left, corner_right, edge, proj_left, proj_right):
+    hbm = pl.BlockSpec(memory_space=pltpu.HBM)
     square = jax.ShapeDtypeStruct((CHI, CHI), F32)
     whole = pltpu.VMEM((UNITS, CHI, CHI), BF16)
     dma = pltpu.SemaphoreType.DMA
     return pl.pallas_call(
         column_kernel,
-        in_specs=[pl.BlockSpec(memory_space=pltpu.SMEM), vmem, vmem, vmem, anywhere, anywhere, anywhere],
-        out_specs=(vmem, vmem, vmem),
+        in_specs=[pl.BlockSpec(memory_space=pltpu.SMEM)] + [hbm] * 8,
+        out_specs=(hbm, hbm, hbm),
         out_shape=(square, square, square),
         scratch_shapes=[
+            pltpu.VMEM((1, UNITS * CHI), jnp.int32),
+            pltpu.VMEM((1, LANES), jnp.int32),
+            pltpu.VMEM((1, LANES), jnp.int32),
+            pltpu.VMEM((64, CHI), F32),
+            pltpu.VMEM((OWNERS, CHI), jnp.int32),
+            pltpu.SMEM((OWNERS, CHI), jnp.int32),
+            pltpu.VMEM((CHI, CHI), BF16),
+            pltpu.VMEM((CHI, CHI), BF16),
             whole, whole, whole,
             pltpu.VMEM((GROUP * CHI, CHI), BF16),
             pltpu.VMEM((CHI, GROUP * CHI), BF16),
@@ -315,6 +350,7 @@
             pltpu.VMEM((2, CAP_TILES * TILE, CHI), BF16),
             pltpu.VMEM((CHI, CHI), F32), pltpu.VMEM((CHI, CHI), F32),
             pltpu.VMEM((CHI, CHI), F32), pltpu.VMEM((CHI, CHI), F32),
+            pltpu.VMEM((CHI, CHI), F32),
             pltpu.VMEM((8, PACKED, HALF), F32),
             pltpu.VMEM((8, PACKED, HALF), F32),
             pltpu.VMEM((8, PACKED, HALF), F32),
@@ -322,36 +358,52 @@
             pltpu.VMEM((6, PACKED, HALF), BF16),
             pltpu.VMEM((PACKED, HALF), BF16),
             pltpu.VMEM((PACKED, HALF), BF16),
-            dma((3, STEPS)), dma((2,)), dma((2,)), dma((8,)), dma((8,)), dma((6,)), dma((6,)), dma, dma,
+            dma((3,)), dma, dma((2,)), dma((2,)),
+            dma((3, STEPS)), dma((2,)), dma((2,)), dma((8,)), dma((8,)), dma((6,)), dma((6,)), dma, dma, dma((3,)),
         ],
         cost_estimate=pl.CostEstimate(flops=9 * 2 * 12800 * 65536, bytes_accessed=24 << 20, transcendentals=0),
         compiler_params=pltpu.CompilerParams(
-            collective_id=0, has_side_effects=True, vmem_limit_bytes=60 * 1024 * 1024
+            collective_id=0, has_side_effects=True, vmem_limit_bytes=58 * 1024 * 1024
         ),
-    )(tiles, dest, from_left, from_right, edge, proj_left, proj_right)
-
-
-def from_behind(value, axis, steps):
-    count = lax.axis_size(axis)
-    pairs = [(source, (source + steps) % count) for source in range(count)]
-    return lax.ppermute(value, axis, pairs)
+    )(sector_owner, row_order, block_size, block_sector, corner_left, corner_right, edge, proj_left, proj_right)
+
+
+def finish_kernel(*refs):
+    copies = [pltpu.make_async_copy(refs[k], refs[3 + k], refs[6].at[k]) for k in range(3)]
+    for copy in copies:
+        copy.start()
+    for copy in copies:
+        copy.wait()
+
+
+def finish(*results):
+    hbm = pl.BlockSpec(memory_space=pltpu.HBM)
+    square = jax.ShapeDtypeStruct((CHI, CHI), F32)
+    return pl.pallas_call(
+        finish_kernel,
+        in_specs=[hbm] * 3,
+        out_specs=(hbm,) * 3,
+        out_shape=(square,) * 3,
+        scratch_shapes=[pltpu.SemaphoreType.DMA((3,))],
+        compiler_params=pltpu.CompilerParams(vmem_limit_bytes=60 * 1024 * 1024),
+    )(*results)
 
 
 def body(
     corner_left, corner_right, edge_top, proj_left, proj_right, row_order, block_size, block_sector, sector_owner,
 ):
-    from_left = from_behind(corner_left, "col", 1)[0, 0]
-    from_right = from_behind(corner_right, "col", -1)[0, 0]
-    dest, tiles = plan(
+    sums = column(
         sector_owner,
-        row_order.reshape(100, LANES),
+        row_order.reshape(1, UNITS * CHI),
         block_size.reshape(1, LANES),
         block_sector.reshape(1, LANES),
-    )
-    edge = jnp.transpose(edge_top[0, 0], (1, 0, 2))
-    left = jnp.transpose(proj_left[0, 0], (1, 0, 2))
-    new_left, new_right, sector_gram = column(tiles, dest, from_left, from_right, edge, left, proj_right[0, 0])
-    return (new_left[None, None], new_right[None, None], sector_gram[None, None])
+        corner_left[0, 0],
+        corner_right[0, 0],
+        jnp.transpose(edge_top[0, 0], (1, 0, 2)),
+        jnp.transpose(proj_left[0, 0], (1, 0, 2)),
+        proj_right[0, 0],
+    )
+    return tuple(out[None, None] for out in finish(*sums))
 
 
 def solution(mesh):

time: 57.3 us -> 71.3 us (1.24)
  Pallas kernels: 41.8 us -> 69.7 us
  local copies, waits for them, and re-layouts: 8.88 us -> 0 us
  starting transfers between devices: 4.2 us -> 0 us
  other arithmetic: 0.93 us -> 0 us
    pallas_call x1, Pallas kernels: 5.07 us -> 25 us  [finish(): pl.pallas_call(finish_kernel, in_specs=[hbm] * 3, out_specs=(hbm,) * 3, o...]
    unnamed x17 -> x0, local copies, waits for them, and re-layouts: 8.88 us -> none
    pallas_call x1, Pallas kernels: 36.7 us -> 44.8 us  [column(): pl.pallas_call(column_kernel, in_specs=[pl.BlockSpec(memory_space=pltpu.S...]
    ppermute x2 -> x0, starting transfers between devices: 4.2 us -> none  [from_behind(): return lax.ppermute(value, axis, pairs)]
    unnamed x1 -> x0, other arithmetic: 0.93 us -> none
  transfers between devices with their start and end apart: 2 -> 0, of which waited for: 0 -> 0; matrix products, arithmetic and copies ran while one was open for 2% -> 0% of each run, Pallas kernels for 9% -> 0%
where the time goes in v3:
time: 71.3 us; the launch traced here: 70.3 us
  Pallas kernels  69.7 us (98%)
    pallas_call x1, Pallas kernels, column(): pl.pallas_call(column_kernel, in_specs=[pl.BlockSpec(memory_space=pltpu.S...  44.8 us
    pallas_call x1, Pallas kernels, finish(): pl.pallas_call(finish_kernel, in_specs=[hbm] * 3, out_specs=(hbm,) * 3, o...  25 us

profile of v3, /device:TPU:0, one launch (start us, length us, event | category | flops | bytes accessed | tf_op | source)
XLA Modules:
  0.0 70.3 jit_solution(6293254563431011005)
XLA Ops:
  0.6 44.8 %shard_map.112 = (f32[256,256]{1,0:T(8,128)}, f32[256,256]{1,0:T(8,128)}, f32[256,256]{1,0:T(8,128)}) custom-call(s32[16]{0:T(128)} %owner_ref.1, s32[1,12800]{1,0:T(1,128)} %bitcast.23, s32[1,128]{1,0:T(1,128)} %bitcast.24, s32[1,128]{1,0:T(1,128)} %bitcast.25, bf16[256,256]{1,0:T(8,128)(2,1)} %bitcast.21, bf16[256,256]{1,0:T(8,128)(2,1)} %bitcast.22, ...), custom_call_target="tpu_custom_call" | custom-call | flops 15099494400 | bytes 25165824 | tf_op jit(solution)/shard_map/pallas_call | solution.py:332
  45.4 25.0 %shard_map.113 = (f32[256,256]{1,0:T(8,128)}, f32[256,256]{1,0:T(8,128)}, f32[256,256]{1,0:T(8,128)}) custom-call(f32[256,256]{1,0:T(8,128)} %get-tuple-element.9.refs_0_, f32[256,256]{1,0:T(8,128)} %get-tuple-element.10.refs_1_, f32[256,256]{1,0:T(8,128)} %get-tuple-element.11.refs_2_), custom_call_target="tpu_custom_call" | custom-call | tf_op jit(solution)/shard_map/pallas_call | solution.py:382

commit v4 on v3

--- a/solution.py
+++ b/solution.py
@@ -369,10 +369,15 @@
 
 
 def finish_kernel(*refs):
-    copies = [pltpu.make_async_copy(refs[k], refs[3 + k], refs[6].at[k]) for k in range(3)]
-    for copy in copies:
+    held, load_sem, store_sem = refs[6:]
+    loads = [pltpu.make_async_copy(refs[k], held.at[k], load_sem.at[k]) for k in range(3)]
+    stores = [pltpu.make_async_copy(held.at[k], refs[3 + k], store_sem.at[k]) for k in range(3)]
+    for copy in loads:
         copy.start()
-    for copy in copies:
+    for k in range(3):
+        loads[k].wait()
+        stores[k].start()
+    for copy in stores:
         copy.wait()
 
 
@@ -384,7 +389,9 @@
         in_specs=[hbm] * 3,
         out_specs=(hbm,) * 3,
         out_shape=(square,) * 3,
-        scratch_shapes=[pltpu.SemaphoreType.DMA((3,))],
+        scratch_shapes=[
+            pltpu.VMEM((3, CHI, CHI), F32), pltpu.SemaphoreType.DMA((3,)), pltpu.SemaphoreType.DMA((3,)),
+        ],
         compiler_params=pltpu.CompilerParams(vmem_limit_bytes=60 * 1024 * 1024),
     )(*results)
 

time: 71.3 us -> 48.3 us (0.68)
  the two profiles are of different devices: /device:TPU:0 before, /device:TPU:32 now
where the time goes in v4:
time: 48.3 us; the launch traced here: 48.1 us
  Pallas kernels  47.5 us (98%)
  between operations  0.64 us (1%)
    pallas_call x1, Pallas kernels, column(): pl.pallas_call(column_kernel, in_specs=[pl.BlockSpec(memory_space=pltpu.S...  45.6 us
    pallas_call x1, Pallas kernels, finish(): pl.pallas_call(finish_kernel, in_specs=[hbm] * 3, out_specs=(hbm,) * 3, o...  1.88 us

profile of v4, /device:TPU:32, one launch (start us, length us, event | category | flops | bytes accessed | tf_op | source)
XLA Modules:
  0.0 48.1 jit_solution(9054036176172056198)
XLA Ops:
  0.6 45.6 %shard_map.112 = (f32[256,256]{1,0:T(8,128)}, f32[256,256]{1,0:T(8,128)}, f32[256,256]{1,0:T(8,128)}) custom-call(s32[16]{0:T(128)} %owner_ref.1, s32[1,12800]{1,0:T(1,128)} %bitcast.23, s32[1,128]{1,0:T(1,128)} %bitcast.24, s32[1,128]{1,0:T(1,128)} %bitcast.25, bf16[256,256]{1,0:T(8,128)(2,1)} %bitcast.21, bf16[256,256]{1,0:T(8,128)(2,1)} %bitcast.22, ...), custom_call_target="tpu_custom_call" | custom-call | flops 15099494400 | bytes 25165824 | tf_op jit(solution)/shard_map/pallas_call | solution.py:332
  46.3 1.9 %shard_map.113 = (f32[256,256]{1,0:T(8,128)}, f32[256,256]{1,0:T(8,128)}, f32[256,256]{1,0:T(8,128)}) custom-call(f32[256,256]{1,0:T(8,128)} %get-tuple-element.9.refs_0_, f32[256,256]{1,0:T(8,128)} %get-tuple-element.10.refs_1_, f32[256,256]{1,0:T(8,128)} %get-tuple-element.11.refs_2_), custom_call_target="tpu_custom_call" | custom-call | tf_op jit(solution)/shard_map/pallas_call | solution.py:387

commit v5 on v4

--- a/solution.py
+++ b/solution.py
@@ -162,7 +162,7 @@
     owner_ref, order_hbm, size_hbm, sector_hbm, left_hbm, right_hbm, edge_hbm, proj_left_hbm, proj_right_hbm,
     out_left, out_right, out_gram,
     order, sizes, sectors, dest, tile_plan, tile_list, from_left, from_right,
-    edge, proj_left, proj_right, enlarged, wide, sorted_rows, listed,
+    edge, proj_left, proj_right, enlarged, wide, sorted_rows, listed_mate, listed_mine,
     left_sum, right_sum, left_other, right_other,
     gram_sum, mine, to_mate, from_mate, to_row, from_row, to_sec, from_sec,
     list_sem, tile_sem, shift_send, shift_recv, load_sem, corner_send, corner_recv, mate_send, mate_recv, row_send, row_recv, sec_send, sec_recv, result_sem,
@@ -192,11 +192,12 @@
     ]
     for copy in lists:
         copy.start()
+    for copy in lists:
+        copy.wait()
     for i in range(STEPS):
         load(0, i).start()
+    for i in range(2):
         load(1, i).start()
-    for i in range(STEPS):
-        load(2, i).start()
 
     pl.semaphore_wait(barrier, len(others))
     shifts = [
@@ -208,8 +209,6 @@
     ]
     for copy in shifts:
         copy.start()
-    for copy in lists:
-        copy.wait()
     plan(owner_ref, order, sizes, sectors, dest, tile_plan)
     tile_copy = pltpu.make_async_copy(tile_plan, tile_list, tile_sem)
     tile_copy.start()
@@ -222,6 +221,12 @@
     def _(i):
         load(0, i).wait()
         load(1, i).wait()
+        load(2, i).start()
+
+        @pl.when(i < STEPS - 2)
+        def _():
+            load(1, i + 2).start()
+
         for j in range(GROUP):
             enlarged[pl.ds(j * CHI, CHI), :] = dot(from_left[...], edge[i * GROUP + j]).astype(BF16)
         chunk = proj_left[pl.ds(i * GROUP, GROUP)].reshape(GROUP * CHI, CHI)
@@ -256,11 +261,13 @@
         source, target = ((left_sum, out_left), (right_sum, out_right), (gram_sum, out_gram))[k]
         return pltpu.make_async_copy(source, target, result_sem.at[k])
 
-    def owner_gram(k, owner):
+    def gather(listed, owner):
         for t in range(CAP_TILES):
             tile = jnp.minimum(jnp.maximum(tile_list[owner, t], 0), UNITS * TILES - 1)
-            listed[k, pl.ds(t * TILE, TILE), :] = sorted_rows[tile]
-        rows = listed[k]
+            listed[pl.ds(t * TILE, TILE), :] = sorted_rows[tile]
+
+    def packed_gram(listed):
+        rows = listed[...]
         return pack(dot_tn(rows, rows))
 
     def mate_copy(i):
@@ -281,19 +288,24 @@
         device_id=partner, device_id_type=MESH,
     )
 
+    def owner_of(i, owner_core):
+        return ((z + 1 + i // 2) % Z_CHIPS) * 4 + owner_core * 2 + (sec + 1 + i) % 2
+
+    gather(listed_mate, owner_of(0, 1 - core))
+
     @pl.loop(0, 2 * Z_CHIPS)
     def _(i):
-        z_owner = (z + 1 + i // 2) % Z_CHIPS
-        sec_owner = (sec + 1 + i) % 2
-        to_mate[i] = owner_gram(0, z_owner * 4 + (1 - core) * 2 + sec_owner)
+        to_mate[i] = packed_gram(listed_mate)
+        gather(listed_mine, owner_of(i, core))
+        mine[i] = packed_gram(listed_mine)
+        gather(listed_mate, owner_of(i + 1, 1 - core))
         mate_copy(i).start()
-        mine[i] = owner_gram(1, z_owner * 4 + core * 2 + sec_owner)
-
-        @pl.when((i >= 1) & (i <= 6))
+
+        @pl.when(i >= 2)
         def _():
-            mate_copy(i - 1).wait_recv()
-            to_row[i - 1] = (mine[i - 1] + from_mate[i - 1]).astype(BF16)
-            row_copy(i - 1).start()
+            mate_copy(i - 2).wait_recv()
+            to_row[i - 2] = (mine[i - 2] + from_mate[i - 2]).astype(BF16)
+            row_copy(i - 2).start()
 
     def column_sum(r):
         mate_copy(6 + r).wait_recv()
@@ -347,7 +359,8 @@
             pltpu.VMEM((GROUP * CHI, CHI), BF16),
             pltpu.VMEM((CHI, GROUP * CHI), BF16),
             pltpu.VMEM((UNITS * TILES, TILE, CHI), BF16),
-            pltpu.VMEM((2, CAP_TILES * TILE, CHI), BF16),
+            pltpu.VMEM((CAP_TILES * TILE, CHI), BF16),
+            pltpu.VMEM((CAP_TILES * TILE, CHI), BF16),
             pltpu.VMEM((CHI, CHI), F32), pltpu.VMEM((CHI, CHI), F32),
             pltpu.VMEM((CHI, CHI), F32), pltpu.VMEM((CHI, CHI), F32),
             pltpu.VMEM((CHI, CHI), F32),

time: 48.3 us -> 46.4 us (0.961)
  the two profiles are of different devices: /device:TPU:32 before, /device:TPU:0 now
where the time goes in v5:
time: 46.4 us; the launch traced here: 46.2 us
  Pallas kernels  45.6 us (98%)
  between operations  0.64 us (1%)
    pallas_call x1, Pallas kernels, column(): pl.pallas_call(column_kernel, in_specs=[pl.BlockSpec(memory_space=pltpu.S...  43.7 us
    pallas_call x1, Pallas kernels, finish(): pl.pallas_call(finish_kernel, in_specs=[hbm] * 3, out_specs=(hbm,) * 3, o...  1.88 us

profile of v5, /device:TPU:0, one launch (start us, length us, event | category | flops | bytes accessed | tf_op | source)
XLA Modules:
  0.0 46.2 jit_solution(1930616231368866873)
XLA Ops:
  0.6 43.7 %shard_map.112 = (f32[256,256]{1,0:T(8,128)}, f32[256,256]{1,0:T(8,128)}, f32[256,256]{1,0:T(8,128)}) custom-call(s32[16]{0:T(128)} %owner_ref.1, s32[1,12800]{1,0:T(1,128)} %bitcast.23, s32[1,128]{1,0:T(1,128)} %bitcast.24, s32[1,128]{1,0:T(1,128)} %bitcast.25, bf16[256,256]{1,0:T(8,128)(2,1)} %bitcast.21, bf16[256,256]{1,0:T(8,128)(2,1)} %bitcast.22, ...), custom_call_target="tpu_custom_call" | custom-call | flops 15099494400 | bytes 25165824 | tf_op jit(solution)/shard_map/pallas_call | solution.py:344
  44.3 1.9 %shard_map.113 = (f32[256,256]{1,0:T(8,128)}, f32[256,256]{1,0:T(8,128)}, f32[256,256]{1,0:T(8,128)}) custom-call(f32[256,256]{1,0:T(8,128)} %get-tuple-element.9.refs_0_, f32[256,256]{1,0:T(8,128)} %get-tuple-element.10.refs_1_, f32[256,256]{1,0:T(8,128)} %get-tuple-element.11.refs_2_), custom_call_target="tpu_custom_call" | custom-call | tf_op jit(solution)/shard_map/pallas_call | solution.py:400

commit v6 on v5

--- a/solution.py
+++ b/solution.py
@@ -68,23 +68,26 @@
     inside = dot(impulses, ones_where(up <= across))
     totals = jnp.broadcast_to(inside[:, LANES - 1:LANES], (112, LANES)).astype(BF16)
     listed = inside + dot(ones_where(iota((112, 112), 1) < iota((112, 112), 0)), totals)
-    bonds = (iota((CHI // TILE, TILE, LANES), 0) * TILE + iota((CHI // TILE, TILE, LANES), 1)).astype(F32).astype(BF16)
-    units = (iota((4, TILE, LANES), 0) * TILE + iota((4, TILE, LANES), 1)).astype(F32).astype(BF16)
+    rows = (iota((LANES // TILE, TILE, LANES), 0) * TILE + iota((LANES // TILE, TILE, LANES), 1)).astype(F32).astype(BF16)
     one, zero = jnp.ones((), BF16), jnp.zeros((), BF16)
-    owned = jnp.zeros((64, CHI), F32)
+    halves = jnp.zeros((LANES, LANES), F32)
     for first in range(0, 100, 20):
         left, right = [], []
         for h in range(first, first + 20):
             order = order_ref[:, h * LANES:(h + 1) * LANES].astype(F32)
-            bond = jnp.floor((order + 0.5) * (1.0 / UNITS))
-            unit = order - UNITS * bond
-            bond, unit, name = (
-                jnp.broadcast_to(x, (TILE, LANES)).astype(BF16)[None] for x in (bond, unit, listed[h:h + 1])
+            pair = jnp.floor((order + 0.5) * (0.5 / UNITS))
+            unit = order - 2 * UNITS * pair
+            unit = jnp.where(unit >= UNITS, unit + (64 - UNITS), unit)
+            pair, unit, name = (
+                jnp.broadcast_to(x, (TILE, LANES)).astype(BF16)[None] for x in (pair, unit, listed[h:h + 1])
             )
-            left.append(jnp.where(units == unit, name, zero).reshape(64, LANES))
-            right.append(jnp.where(bonds == bond, one, zero).reshape(CHI, LANES))
-        owned = owned + dot_nt(jnp.concatenate(left, axis=1), jnp.concatenate(right, axis=1))
-    return owned
+            left.append(jnp.where(rows == unit, name, zero).reshape(LANES, LANES))
+            right.append(jnp.where(rows == pair, one, zero).reshape(LANES, LANES))
+        halves = halves + dot_nt(jnp.concatenate(left, axis=1), jnp.concatenate(right, axis=1))
+    halves = halves.astype(BF16)
+    up, across = iota((CHI, CHI), 0), iota((CHI, CHI), 1)
+    weave = ones_where(across == jnp.where(up < LANES, 2 * up, 2 * (up - LANES) + 1))
+    return dot(jnp.concatenate([halves[:64], halves[64:]], axis=1), weave)
 
 
 def plan(owner_ref, order_ref, size_ref, sector_ref, dest_ref, tile_ref):
@@ -164,14 +167,16 @@
     order, sizes, sectors, dest, tile_plan, tile_list, from_left, from_right,
     edge, proj_left, proj_right, enlarged, wide, sorted_rows, listed_mate, listed_mine,
     left_sum, right_sum, left_other, right_other,
-    gram_sum, mine, to_mate, from_mate, to_row, from_row, to_sec, from_sec,
-    list_sem, tile_sem, shift_send, shift_recv, load_sem, corner_send, corner_recv, mate_send, mate_recv, row_send, row_recv, sec_send, sec_recv, result_sem,
+    gram_sum, mine, to_mate, from_mate, to_row, from_row,
+    list_sem, tile_sem, shift_send, shift_recv, load_sem, corner_send, corner_recv, mate_send, mate_recv, row_send, row_recv, result_sem,
 ):
     col, row, sec = lax.axis_index("col"), lax.axis_index("row"), lax.axis_index("sec")
     z, core = row // 2, row % 2
     mate = {"row": z * 2 + (1 - core)}
     partner = {"sec": 1 - sec}
-    ahead = [{"row": ((z + dz) % Z_CHIPS) * 2 + core} for dz in range(1, Z_CHIPS)]
+    ahead = [
+        {"row": ((z + dz) % Z_CHIPS) * 2 + core, "sec": side} for dz in range(1, Z_CHIPS) for side in (sec, 1 - sec)
+    ]
 
     sides = [{"col": (col + 1) % 8}, {"col": (col + 7) % 8}]
     others = [mate, partner] + ahead + sides
@@ -192,14 +197,6 @@
     ]
     for copy in lists:
         copy.start()
-    for copy in lists:
-        copy.wait()
-    for i in range(STEPS):
-        load(0, i).start()
-    for i in range(2):
-        load(1, i).start()
-
-    pl.semaphore_wait(barrier, len(others))
     shifts = [
         pltpu.make_async_remote_copy(
             src_ref=source, dst_ref=target, send_sem=shift_send.at[k], recv_sem=shift_recv.at[k],
@@ -207,35 +204,21 @@
         )
         for k, (source, target) in enumerate(((left_hbm, from_left), (right_hbm, from_right)))
     ]
-    for copy in shifts:
-        copy.start()
+    pl.semaphore_wait(barrier, len(others))
+    shifts[0].start()
+    for copy in lists:
+        copy.wait()
+    for i in range(STEPS):
+        load(0, i).start()
+        if i < 2:
+            load(1, i).start()
+
     plan(owner_ref, order, sizes, sectors, dest, tile_plan)
+    shifts[1].start()
     tile_copy = pltpu.make_async_copy(tile_plan, tile_list, tile_sem)
     tile_copy.start()
-    shifts[0].wait()
-
     left_sum[...] = jnp.zeros_like(left_sum)
     right_sum[...] = jnp.zeros_like(right_sum)
-
-    @pl.loop(0, STEPS)
-    def _(i):
-        load(0, i).wait()
-        load(1, i).wait()
-        load(2, i).start()
-
-        @pl.when(i < STEPS - 2)
-        def _():
-            load(1, i + 2).start()
-
-        for j in range(GROUP):
-            enlarged[pl.ds(j * CHI, CHI), :] = dot(from_left[...], edge[i * GROUP + j]).astype(BF16)
-        chunk = proj_left[pl.ds(i * GROUP, GROUP)].reshape(GROUP * CHI, CHI)
-        left_sum[...] += dot_tn(chunk, enlarged[...])
-        for j in range(GROUP):
-            u = i * GROUP + j
-            ordered = dot(sort_matrix(dest[pl.ds(u, 1), :]), enlarged[pl.ds(j * CHI, CHI), :])
-            sorted_rows[pl.ds(u * TILES, TILES)] = ordered.astype(BF16).reshape(TILES, TILE, CHI)
-
     def corner_copy(k):
         source, target = ((left_sum, left_other), (right_sum, right_other))[k]
         return pltpu.make_async_remote_copy(
@@ -243,7 +226,81 @@
             device_id=partner, device_id_type=MESH,
         )
 
+    shifts[0].wait()
+
+    @pl.loop(0, STEPS)
+    def _(i):
+        load(0, i).wait()
+        load(1, i).wait()
+        load(2, i).start()
+
+        @pl.when(i < STEPS - 2)
+        def _():
+            load(1, i + 2).start()
+
+        part = pl.ds(i * GROUP, GROUP)
+        for j in range(GROUP):
+            enlarged[i * GROUP + j] = dot(from_left[...], edge[i * GROUP + j]).astype(BF16)
+        left_sum[...] += dot_tn(proj_left[part].reshape(GROUP * CHI, CHI), enlarged[part].reshape(GROUP * CHI, CHI))
+        for j in range(GROUP):
+            u = i * GROUP + j
+            ordered = dot(sort_matrix(dest[pl.ds(u, 1), :]), enlarged[u])
+            sorted_rows[pl.ds(u * TILES, TILES)] = ordered.astype(BF16).reshape(TILES, TILE, CHI)
+
     corner_copy(0).start()
+    def result(k):
+        source, target = ((left_sum, out_left), (right_sum, out_right), (gram_sum, out_gram))[k]
+        return pltpu.make_async_copy(source, target, result_sem.at[k])
+
+    def gather(listed, owner):
+        for t in range(CAP_TILES):
+            tile = jnp.minimum(jnp.maximum(tile_list[owner, t], 0), UNITS * TILES - 1)
+            listed[pl.ds(t * TILE, TILE), :] = sorted_rows[tile]
+
+    def packed_gram(listed):
+        rows = listed[...]
+        return pack(dot_tn(rows, rows))
+
+    def mate_copy(i):
+        return pltpu.make_async_remote_copy(
+            src_ref=to_mate.at[i], dst_ref=from_mate.at[i], send_sem=mate_send.at[i], recv_sem=mate_recv.at[i],
+            device_id=mate, device_id_type=MESH,
+        )
+
+    def row_copy(j):
+        target = {"row": ((z + 1 + j) % Z_CHIPS) * 2 + core, "sec": (sec + 1 + j // Z_CHIPS) % 2}
+        return pltpu.make_async_remote_copy(
+            src_ref=to_row.at[j], dst_ref=from_row.at[j], send_sem=row_send.at[j], recv_sem=row_recv.at[j],
+            device_id=target, device_id_type=MESH,
+        )
+
+    def owner_of(i, owner_core):
+        return ((z + 1 + i) % Z_CHIPS) * 4 + owner_core * 2 + (sec + 1 + i // Z_CHIPS) % 2
+
+    def forward(j):
+        mate_copy(j).wait_recv()
+        to_row[j] = (mine[j] + from_mate[j]).astype(BF16)
+        row_copy(j).start()
+
+    tile_copy.wait()
+    gather(listed_mate, owner_of(0, 1 - core))
+    to_mate[0] = packed_gram(listed_mate)
+    gather(listed_mine, owner_of(1, 1 - core))
+    mate_copy(0).start()
+    to_mate[1] = packed_gram(listed_mine)
+    gather(listed_mine, owner_of(0, core))
+    gather(listed_mate, owner_of(2, 1 - core))
+    mate_copy(1).start()
+
+    def gram_step(i):
+        mine[i] = packed_gram(listed_mine)
+        gather(listed_mine, owner_of(i + 1, core))
+        to_mate[i + 2] = packed_gram(listed_mate)
+        gather(listed_mate, owner_of(i + 3, 1 - core))
+        mate_copy(i + 2).start()
+        forward(i)
+
+    pl.loop(0, 2)(gram_step)
     shifts[1].wait()
 
     @pl.loop(0, STEPS)
@@ -251,87 +308,31 @@
         load(2, i).wait()
         for j in range(GROUP):
             wide[:, pl.ds(j * CHI, CHI)] = dot(edge[i * GROUP + j], from_right[...]).astype(BF16)
-        chunk = proj_right[pl.ds(i * GROUP, GROUP)].reshape(GROUP * CHI, CHI)
-        right_sum[...] += dot(wide[...], chunk)
+        right_sum[...] += dot(wide[...], proj_right[pl.ds(i * GROUP, GROUP)].reshape(GROUP * CHI, CHI))
 
     corner_copy(1).start()
-    tile_copy.wait()
-
-    def result(k):
-        source, target = ((left_sum, out_left), (right_sum, out_right), (gram_sum, out_gram))[k]
-        return pltpu.make_async_copy(source, target, result_sem.at[k])
-
-    def gather(listed, owner):
-        for t in range(CAP_TILES):
-            tile = jnp.minimum(jnp.maximum(tile_list[owner, t], 0), UNITS * TILES - 1)
-            listed[pl.ds(t * TILE, TILE), :] = sorted_rows[tile]
-
-    def packed_gram(listed):
-        rows = listed[...]
-        return pack(dot_tn(rows, rows))
-
-    def mate_copy(i):
-        return pltpu.make_async_remote_copy(
-            src_ref=to_mate.at[i], dst_ref=from_mate.at[i], send_sem=mate_send.at[i], recv_sem=mate_recv.at[i],
-            device_id=mate, device_id_type=MESH,
-        )
-
-    def row_copy(j):
-        target = {"row": ((z + 1 + j // 2) % Z_CHIPS) * 2 + core}
-        return pltpu.make_async_remote_copy(
-            src_ref=to_row.at[j], dst_ref=from_row.at[j], send_sem=row_send.at[j], recv_sem=row_recv.at[j],
-            device_id=target, device_id_type=MESH,
-        )
-
-    sec_copy = pltpu.make_async_remote_copy(
-        src_ref=to_sec, dst_ref=from_sec, send_sem=sec_send, recv_sem=sec_recv,
-        device_id=partner, device_id_type=MESH,
-    )
-
-    def owner_of(i, owner_core):
-        return ((z + 1 + i // 2) % Z_CHIPS) * 4 + owner_core * 2 + (sec + 1 + i) % 2
-
-    gather(listed_mate, owner_of(0, 1 - core))
-
-    @pl.loop(0, 2 * Z_CHIPS)
-    def _(i):
-        to_mate[i] = packed_gram(listed_mate)
-        gather(listed_mine, owner_of(i, core))
-        mine[i] = packed_gram(listed_mine)
-        gather(listed_mate, owner_of(i + 1, 1 - core))
-        mate_copy(i).start()
-
-        @pl.when(i >= 2)
-        def _():
-            mate_copy(i - 2).wait_recv()
-            to_row[i - 2] = (mine[i - 2] + from_mate[i - 2]).astype(BF16)
-            row_copy(i - 2).start()
-
-    def column_sum(r):
-        mate_copy(6 + r).wait_recv()
-        total = mine[6 + r] + from_mate[6 + r]
-        for k in range(Z_CHIPS - 1):
-            row_copy(2 * k + r).wait_recv()
-            total = total + from_row[2 * k + r].astype(F32)
-        return total
-
-    to_sec[...] = column_sum(0).astype(BF16)
-    sec_copy.start()
+    pl.loop(2, 6)(gram_step)
+    mine[6] = packed_gram(listed_mine)
+    gather(listed_mate, owner_of(7, core))
+    forward(6)
+    mine[7] = packed_gram(listed_mate)
+    corner_copy(1).wait()
+    right_sum[...] = normalized(right_sum[...] + right_other[...])
+    result(1).start()
+    mate_copy(7).wait_recv()
+    total = mine[7] + from_mate[7]
     corner_copy(0).wait()
     left_sum[...] = normalized(left_sum[...] + left_other[...])
     result(0).start()
-    corner_copy(1).wait()
-    right_sum[...] = normalized(right_sum[...] + right_other[...])
-    result(1).start()
-    total = column_sum(1)
-    sec_copy.wait_recv()
-    gram_sum[...] = unpack(total + from_sec[...].astype(F32))
+    for j in range(7):
+        row_copy(j).wait_recv()
+        total = total + from_row[j].astype(F32)
+    gram_sum[...] = unpack(total)
     result(2).start()
     for i in range(2 * Z_CHIPS):
         mate_copy(i).wait_send()
-    for j in range(2 * (Z_CHIPS - 1)):
+    for j in range(7):
         row_copy(j).wait_send()
-    sec_copy.wait_send()
     for k in range(3):
         result(k).wait()
 
@@ -355,8 +356,7 @@
             pltpu.SMEM((OWNERS, CHI), jnp.int32),
             pltpu.VMEM((CHI, CHI), BF16),
             pltpu.VMEM((CHI, CHI), BF16),
-            whole, whole, whole,
-            pltpu.VMEM((GROUP * CHI, CHI), BF16),
+            whole, whole, whole, whole,
             pltpu.VMEM((CHI, GROUP * CHI), BF16),
             pltpu.VMEM((UNITS * TILES, TILE, CHI), BF16),
             pltpu.VMEM((CAP_TILES * TILE, CHI), BF16),
@@ -367,12 +367,10 @@
             pltpu.VMEM((8, PACKED, HALF), F32),
             pltpu.VMEM((8, PACKED, HALF), F32),
             pltpu.VMEM((8, PACKED, HALF), F32),
-            pltpu.VMEM((6, PACKED, HALF), BF16),
-            pltpu.VMEM((6, PACKED, HALF), BF16),
-            pltpu.VMEM((PACKED, HALF), BF16),
-            pltpu.VMEM((PACKED, HALF), BF16),
+            pltpu.VMEM((7, PACKED, HALF), BF16),
+            pltpu.VMEM((7, PACKED, HALF), BF16),
             dma((3,)), dma, dma((2,)), dma((2,)),
-            dma((3, STEPS)), dma((2,)), dma((2,)), dma((8,)), dma((8,)), dma((6,)), dma((6,)), dma, dma, dma((3,)),
+            dma((3, STEPS)), dma((2,)), dma((2,)), dma((8,)), dma((8,)), dma((7,)), dma((7,)), dma((3,)),
         ],
         cost_estimate=pl.CostEstimate(flops=9 * 2 * 12800 * 65536, bytes_accessed=24 << 20, transcendentals=0),
         compiler_params=pltpu.CompilerParams(

time: 46.4 us -> 45.3 us (0.976)
  Pallas kernels: 45.6 us -> 44.5 us
    pallas_call x1, Pallas kernels: 43.7 us -> 42.6 us  [column(): pl.pallas_call(column_kernel, in_specs=[pl.BlockSpec(memory_space=pltpu.S...]
where the time goes in v6:
time: 45.3 us; the launch traced here: 45.1 us
  Pallas kernels  44.5 us (98%)
  between operations  0.64 us (1%)
    pallas_call x1, Pallas kernels, column(): pl.pallas_call(column_kernel, in_specs=[pl.BlockSpec(memory_space=pltpu.S...  42.6 us
    pallas_call x1, Pallas kernels, finish(): pl.pallas_call(finish_kernel, in_specs=[hbm] * 3, out_specs=(hbm,) * 3, o...  1.88 us

profile of v6, /device:TPU:0, one launch (start us, length us, event | category | flops | bytes accessed | tf_op | source)
XLA Modules:
  0.0 45.1 jit_solution(10787539696962458551)
XLA Ops:
  0.6 42.6 %shard_map.112 = (f32[256,256]{1,0:T(8,128)}, f32[256,256]{1,0:T(8,128)}, f32[256,256]{1,0:T(8,128)}) custom-call(s32[16]{0:T(128)} %owner_ref.1, s32[1,12800]{1,0:T(1,128)} %bitcast.23, s32[1,128]{1,0:T(1,128)} %bitcast.24, s32[1,128]{1,0:T(1,128)} %bitcast.25, bf16[256,256]{1,0:T(8,128)(2,1)} %bitcast.21, bf16[256,256]{1,0:T(8,128)(2,1)} %bitcast.22, ...), custom_call_target="tpu_custom_call" | custom-call | flops 15099494400 | bytes 25165824 | tf_op jit(solution)/shard_map/pallas_call | solution.py:345
  43.2 1.9 %shard_map.113 = (f32[256,256]{1,0:T(8,128)}, f32[256,256]{1,0:T(8,128)}, f32[256,256]{1,0:T(8,128)}) custom-call(f32[256,256]{1,0:T(8,128)} %get-tuple-element.9.refs_0_, f32[256,256]{1,0:T(8,128)} %get-tuple-element.10.refs_1_, f32[256,256]{1,0:T(8,128)} %get-tuple-element.11.refs_2_), custom_call_target="tpu_custom_call" | custom-call | tf_op jit(solution)/shard_map/pallas_call | solution.py:398

commit v7 on v6

--- a/solution.py
+++ b/solution.py
@@ -14,6 +14,7 @@
 TILE = 16
 TILES = 32
 CAP_TILES = 144
+HELD = 2048
 EMPTY = TILES - 1
 GROUP = 10
 STEPS = UNITS // GROUP
@@ -179,7 +180,7 @@
     ]
 
     sides = [{"col": (col + 1) % 8}, {"col": (col + 7) % 8}]
-    others = [mate, partner] + ahead + sides
+    others = sides + [mate, partner] + ahead
 
     barrier = pltpu.get_barrier_semaphore()
     for other in others:
@@ -254,7 +255,7 @@
 
     def gather(listed, owner):
         for t in range(CAP_TILES):
-            tile = jnp.minimum(jnp.maximum(tile_list[owner, t], 0), UNITS * TILES - 1)
+            tile = tile_list[owner, t] & (HELD - 1)
             listed[pl.ds(t * TILE, TILE), :] = sorted_rows[tile]
 
     def packed_gram(listed):
@@ -300,7 +301,7 @@
         mate_copy(i + 2).start()
         forward(i)
 
-    pl.loop(0, 2)(gram_step)
+    pl.loop(0, 4)(gram_step)
     shifts[1].wait()
 
     @pl.loop(0, STEPS)
@@ -311,7 +312,7 @@
         right_sum[...] += dot(wide[...], proj_right[pl.ds(i * GROUP, GROUP)].reshape(GROUP * CHI, CHI))
 
     corner_copy(1).start()
-    pl.loop(2, 6)(gram_step)
+    pl.loop(4, 6)(gram_step)
     mine[6] = packed_gram(listed_mine)
     gather(listed_mate, owner_of(7, core))
     forward(6)
@@ -358,7 +359,7 @@
             pltpu.VMEM((CHI, CHI), BF16),
             whole, whole, whole, whole,
             pltpu.VMEM((CHI, GROUP * CHI), BF16),
-            pltpu.VMEM((UNITS * TILES, TILE, CHI), BF16),
+            pltpu.VMEM((HELD, TILE, CHI), BF16),
             pltpu.VMEM((CAP_TILES * TILE, CHI), BF16),
             pltpu.VMEM((CAP_TILES * TILE, CHI), BF16),
             pltpu.VMEM((CHI, CHI), F32), pltpu.VMEM((CHI, CHI), F32),

time: 45.3 us -> 45.3 us (level)
  no operation moved by 1% of the time
where the time goes in v7:
time: 45.3 us; the launch traced here: 44.8 us
  Pallas kernels  44.1 us (97%)
  between operations  0.64 us (1%)
    pallas_call x1, Pallas kernels, column(): pl.pallas_call(column_kernel, in_specs=[pl.BlockSpec(memory_space=pltpu.S...  42.2 us
    pallas_call x1, Pallas kernels, finish(): pl.pallas_call(finish_kernel, in_specs=[hbm] * 3, out_specs=(hbm,) * 3, o...  1.88 us

profile of v7, /device:TPU:0, one launch (start us, length us, event | category | flops | bytes accessed | tf_op | source)
XLA Modules:
  0.0 44.8 jit_solution(15531220624223619063)
XLA Ops:
  0.6 42.2 %shard_map.112 = (f32[256,256]{1,0:T(8,128)}, f32[256,256]{1,0:T(8,128)}, f32[256,256]{1,0:T(8,128)}) custom-call(s32[16]{0:T(128)} %owner_ref.1, s32[1,12800]{1,0:T(1,128)} %bitcast.23, s32[1,128]{1,0:T(1,128)} %bitcast.24, s32[1,128]{1,0:T(1,128)} %bitcast.25, bf16[256,256]{1,0:T(8,128)(2,1)} %bitcast.21, bf16[256,256]{1,0:T(8,128)(2,1)} %bitcast.22, ...), custom_call_target="tpu_custom_call" | custom-call | flops 15099494400 | bytes 25165824 | tf_op jit(solution)/shard_map/pallas_call | solution.py:346
  42.9 1.9 %shard_map.113 = (f32[256,256]{1,0:T(8,128)}, f32[256,256]{1,0:T(8,128)}, f32[256,256]{1,0:T(8,128)}) custom-call(f32[256,256]{1,0:T(8,128)} %get-tuple-element.9.refs_0_, f32[256,256]{1,0:T(8,128)} %get-tuple-element.10.refs_1_, f32[256,256]{1,0:T(8,128)} %get-tuple-element.11.refs_2_), custom_call_target="tpu_custom_call" | custom-call | tf_op jit(solution)/shard_map/pallas_call | solution.py:399

commit v8 on v6

--- a/solution.py
+++ b/solution.py
@@ -300,7 +300,7 @@
         mate_copy(i + 2).start()
         forward(i)
 
-    pl.loop(0, 2)(gram_step)
+    pl.loop(0, 3)(gram_step)
     shifts[1].wait()
 
     @pl.loop(0, STEPS)
@@ -311,24 +311,24 @@
         right_sum[...] += dot(wide[...], proj_right[pl.ds(i * GROUP, GROUP)].reshape(GROUP * CHI, CHI))
 
     corner_copy(1).start()
-    pl.loop(2, 6)(gram_step)
+    pl.loop(3, 6)(gram_step)
+    corner_copy(0).wait()
+    left_sum[...] = normalized(left_sum[...] + left_other[...])
+    result(0).start()
     mine[6] = packed_gram(listed_mine)
     gather(listed_mate, owner_of(7, core))
     forward(6)
     mine[7] = packed_gram(listed_mate)
-    corner_copy(1).wait()
-    right_sum[...] = normalized(right_sum[...] + right_other[...])
-    result(1).start()
     mate_copy(7).wait_recv()
     total = mine[7] + from_mate[7]
-    corner_copy(0).wait()
-    left_sum[...] = normalized(left_sum[...] + left_other[...])
-    result(0).start()
     for j in range(7):
         row_copy(j).wait_recv()
         total = total + from_row[j].astype(F32)
     gram_sum[...] = unpack(total)
     result(2).start()
+    corner_copy(1).wait()
+    right_sum[...] = normalized(right_sum[...] + right_other[...])
+    result(1).start()
     for i in range(2 * Z_CHIPS):
         mate_copy(i).wait_send()
     for j in range(7):

time: 45.3 us -> 44.9 us (level)
  no operation moved by 1% of the time
where the time goes in v8:
time: 44.9 us; the launch traced here: 44.8 us
  Pallas kernels  44.1 us (98%)
  between operations  0.64 us (1%)
    pallas_call x1, Pallas kernels, column(): pl.pallas_call(column_kernel, in_specs=[pl.BlockSpec(memory_space=pltpu.S...  42.2 us
    pallas_call x1, Pallas kernels, finish(): pl.pallas_call(finish_kernel, in_specs=[hbm] * 3, out_specs=(hbm,) * 3, o...  1.88 us

profile of v8, /device:TPU:0, one launch (start us, length us, event | category | flops | bytes accessed | tf_op | source)
XLA Modules:
  0.0 44.8 jit_solution(1674990609063863744)
XLA Ops:
  0.6 42.2 %shard_map.112 = (f32[256,256]{1,0:T(8,128)}, f32[256,256]{1,0:T(8,128)}, f32[256,256]{1,0:T(8,128)}) custom-call(s32[16]{0:T(128)} %owner_ref.1, s32[1,12800]{1,0:T(1,128)} %bitcast.23, s32[1,128]{1,0:T(1,128)} %bitcast.24, s32[1,128]{1,0:T(1,128)} %bitcast.25, bf16[256,256]{1,0:T(8,128)(2,1)} %bitcast.21, bf16[256,256]{1,0:T(8,128)(2,1)} %bitcast.22, ...), custom_call_target="tpu_custom_call" | custom-call | flops 15099494400 | bytes 25165824 | tf_op jit(solution)/shard_map/pallas_call | solution.py:345
  42.9 1.9 %shard_map.113 = (f32[256,256]{1,0:T(8,128)}, f32[256,256]{1,0:T(8,128)}, f32[256,256]{1,0:T(8,128)}) custom-call(f32[256,256]{1,0:T(8,128)} %get-tuple-element.9.refs_0_, f32[256,256]{1,0:T(8,128)} %get-tuple-element.10.refs_1_, f32[256,256]{1,0:T(8,128)} %get-tuple-element.11.refs_2_), custom_call_target="tpu_custom_call" | custom-call | tf_op jit(solution)/shard_map/pallas_call | solution.py:398
